TPU v7x, 32 devices: a whole 2x2x4 slice. The times are simulated.
32 devices in a mesh: grp: 2 (over y), wave: 4 (over z), lat: 4 (over x, core).
Axes of the slice: x: 2, y: 2, z: 4, core: 2. Of those that a mesh axis runs over, the one named last changes fastest.
Arguments:
- fourier: bfloat16 [5120, 8192], P(('grp', 'lat', 'wave')), parts along dimension 0, may hold values from -6 to 6
- row_points: int32 [2560], P(('lat', 'wave')), may hold values from 20 to 5260, as said below
- owner_order: int32 [16], replicated, may hold values from 0 to 15, each once
- gauss_weight: float32 [2560], P('lat'), may hold values from 0.5 to 2
- table: bfloat16 [16, 2560, 1280], P('wave', 'lat'), may hold values from -0.125 to 0.125
Outputs:
- spectral: float32 [2560, 8192], P(('grp', 'lat'), 'wave'), parts along dimension 0
There are 2 independent parts, one for each index of `grp`. A program takes and returns all parts, laid end to end along the dimension named above; an argument that names none is the same for every part. Nothing has to cross between parts.
Inputs may be any that keep to these rules, and one draw needn't show every extreme that they name: `row_points`: row lengths of an octahedral reduced grid, 20 + 4 min(j, 2559 - j) points, plus 4 times a per-row extra of 0 to 31; the first row has no extra and row 1279 the most.
All inputs are finite; a program needn't handle non-finite values.
Results may differ from a plain program's by a relative error of at most 0.0029.
Values may be sent and summed in bfloat16 or wider, within the bound.
No kernel may reach another device: no remote copies, remote signals or barrier semaphores. Data moves between devices by JAX's collectives and lax.ppermute only.
A program may use at most 128 MiB of HBM per device.

v0:
```python
import jax
import jax.numpy as jnp
from jax import lax
from jax.sharding import PartitionSpec as P


def per_device(fourier, row_points, owner_order, gauss_weight, table):
    slot_total = owner_order.shape[0]
    own_slots, band_count, degrees = table.shape
    stride = degrees // slot_total
    local_rows = fourier.shape[0]
    columns = fourier.shape[1] // slot_total
    wave_numbers = jnp.arange(slot_total, dtype=jnp.int32) * stride
    kept_mask = wave_numbers[None, :] < (row_points // 2)[:, None]
    spread = fourier.reshape(local_rows, slot_total, columns)
    spread = jnp.where(kept_mask[:, :, None], spread, jnp.zeros((), jnp.bfloat16))
    ordered = jnp.take(spread, owner_order, axis=1).reshape(local_rows, slot_total * columns)
    band_rows = lax.all_to_all(ordered, "wave", split_axis=1, concat_axis=0, tiled=True)
    weighted = (gauss_weight[:, None] * band_rows.astype(jnp.float32)).astype(jnp.bfloat16)
    weighted = weighted.reshape(band_count, own_slots, columns)
    share = degrees // lax.axis_size("lat")
    product = jnp.einsum("sjn,jsc->nsc", table, weighted, preferred_element_type=jnp.float32)
    totals = lax.psum_scatter(
        product.reshape(degrees, own_slots * columns), "lat", scatter_dimension=0, tiled=True
    )
    first_degree = lax.axis_index("lat") * share
    degree = first_degree + jnp.arange(share, dtype=jnp.int32)
    slot_wave = (
        lax.dynamic_slice_in_dim(owner_order, lax.axis_index("wave") * own_slots, own_slots)
        * stride
    )
    alive_mask = degree[:, None] >= slot_wave[None, :]
    shaped = totals.reshape(share, own_slots, columns)
    result = jnp.where(alive_mask[:, :, None], shaped, jnp.zeros((), jnp.float32))
    return result.reshape(share, own_slots * columns)


def solution(mesh):
    in_specs = (
        P(("grp", "lat", "wave"), None),
        P(("lat", "wave")),
        P(),
        P("lat"),
        P("wave", "lat", None),
    )
    out_specs = P(("grp", "lat"), "wave")
    return jax.shard_map(
        per_device, mesh=mesh, in_specs=in_specs, out_specs=out_specs, check_vma=False
    )
```

profile of v0, /device:TPU:0, one launch (start us, length us, event | category | flops | bytes accessed | tf_op | source)
XLA Modules:
  0.0 221.1 jit_solution(10807706027441914864)
XLA Ops:
  6.5 0.7 compare_and_fusion
  7.2 0.7 compare_select_fusion
  7.9 0.1 broadcast_in_dim.53
  7.9 0.7 and_select_fusion
  8.6 0.1 broadcast_bitcast_fusion
  8.8 3.1 %bitcast_select_fusion = bf16[160,16,512]{2,0,1:T(8,128)(2,1)} fusion(bf16[20,16,8,512]{3,2,1,0:T(8,128)(2,1)} %bitcast.18, pred[160,16]{0,1:T(8,128)(4,1)S(1)} %broadcast_compare_fusion.1), kind=kLoop, calls=%fused_computation.3 | loop fusion | flops 1310720 | bytes 5245440 | tf_op jit(solution)/shard_map/jit(_where)/select_n | solution.py:16
  11.9 2.5 %gather_fusion = bf16[16,160,512]{2,1,0:T(8,128)(2,1)S(1)} fusion(bf16[160,16,512]{2,0,1:T(8,128)(2,1)} %bitcast_select_fusion, s32[1024]{0:T(1024)S(1)} %pad_clamp_fusion), kind=kCustom, calls=%fused_computation | custom fusion | bytes 5242944 | tf_op jit(solution)/shard_map/jit(_take)/gather | solution.py:17
  14.3 2.9 %copy.17 = bf16[160,16,512]{2,1,0:T(8,128)(2,1)} copy(bf16[160,16,512]{2,0,1:T(8,128)(2,1)S(1)} %bitcast.16) | data formatting | bytes 5242880 | tf_op jit(solution)/shard_map/jit(_take)/gather | solution.py:17
  17.3 4.2 %gather.7 = bf16[160,4,2048]{2,1,0:T(4,128)(2,1)S(1)} reshape(bf16[160,16,512]{2,1,0:T(8,128)(2,1)} %copy.17) | data formatting | bytes 5242880 | tf_op jit(solution)/shard_map/jit(_take)/gather | solution.py:17
  21.4 1.1 broadcast_select_fusion
  22.6 1.4 copy.18
  24.0 65.6 %all_to_all.10 = bf16[160,4,2048]{2,0,1:T(8,128)(2,1)S(1)} all-to-all(bf16[160,4,2048]{2,0,1:T(8,128)(2,1)S(1)} %copy.18), channel_id=1, replica_groups=mesh['grp'=2,'wave'=4,'lat'=4] {'wave'}, dimensions={1} | all-to-all | bytes 5242880 | tf_op jit(solution)/shard_map/all_to_all | solution.py:18
  89.6 3.0 %convert_bitcast_fusion = f32[4,160,2048]{2,1,0:T(8,128)} fusion(bf16[160,4,2048]{2,0,1:T(8,128)(2,1)S(1)} %all_to_all.10), kind=kLoop, calls=%fused_computation.1 | loop fusion | flops 1310720 | bytes 7864320 | tf_op jit(solution)/shard_map/convert_element_type | solution.py:19
  92.6 7.6 %reshape.102 = f32[640,4,512]{2,1,0:T(4,128)} reshape(f32[4,160,2048]{2,1,0:T(8,128)} %convert_bitcast_fusion) | data formatting | bytes 10485760 | tf_op jit(solution)/shard_map/convert_element_type | solution.py:19
  100.2 4.3 %multiply_convert_fusion = bf16[640,4,512]{2,1,0:T(4,128)(2,1)S(1)} fusion(f32[640,4,512]{2,1,0:T(4,128)} %reshape.102, f32[640]{0:T(1024)S(1)} %copy-done), kind=kLoop, calls=%fused_computation.2 | loop fusion | flops 2621440 | bytes 7866880 | tf_op jit(solution)/shard_map/convert_element_type | solution.py:19
  104.4 9.9 %fusion = f32[4,512,1280]{2,1,0:T(8,128)} fusion(bf16[4,640,1280]{2,1,0:T(8,128)(2,1)} %param.9, bf16[640,4,512]{2,1,0:T(4,128)(2,1)S(1)} %multiply_convert_fusion), kind=kOutput, calls=%fused_computation.4 | convolution fusion | flops 3355443200 | bytes 19660800 | tf_op jit(solution)/shard_map/sjn,jsc->nsc/dot_general | solution.py:22
  114.4 11.4 %copy.20 = f32[1280,2048]{1,0:T(8,128)} copy(f32[1280,2048]{0,1:T(8,128)} %bitcast.15) | data formatting | bytes 20971520 | tf_op jit(solution)/shard_map/reshape | solution.py:24
  125.8 0.6 copy-done.1
  126.4 0.1 dynamic-slice_multiply_fusion
  126.5 0.1 broadcast_compare_fusion
  126.6 0.5 broadcast_in_dim.51
  127.1 0.4 copy.22
  127.5 83.0 %reduce-scatter.2.cloned.1.call-done = f32[320,2048]{1,0:T(8,128)} async-done(((f32[1280,2048]{1,0:T(8,128)}), f32[320,2048]{1,0:T(8,128)}) %reduce-scatter.2.cloned.1.call-update) | async-done | bytes 2621456 | tf_op jit(solution)/shard_map/reduce_scatter | solution.py:23
  210.5 3.7 %broadcast_select_fusion.1 = f32[320,2048]{1,0:T(8,128)} fusion(pred[320,2048]{1,0:T(8,128)(4,1)S(1)} %bitcast.19, f32[320,2048]{1,0:T(8,128)} %reduce-scatter.2.cloned.1.call-done), kind=kLoop, calls=%fused_computation.7 | loop fusion | flops 655360 | bytes 5898240 | tf_op jit(solution)/shard_map/jit(_where)/select_n | solution.py:34
  (10 shorter events, 0.1 us)
Async XLA Ops:
  6.5 204.0 %reduce-scatter.2.cloned.1.call-start = ((), (), s32[]{:S(2)}) async-start(), calls=%async_computation.2 | async-start | bytes 13107200 | tf_op jit(solution)/shard_map/reduce_scatter | solution.py:23
  92.6 7.6 %copy-start = (f32[640]{0:T(1024)S(1)}, f32[640]{0:T(1024)}, u32[]{:S(2)}) copy-start(f32[640]{0:T(1024)} %param.8) | copy-start | bytes 7684
  125.7 0.7 copy-start.1
Sparse Core Ops, SparseCore 0:
  125.9 84.5 reduce-scatter.1
where the time goes:
time: 222 us; the launch traced here: 221 us
  waiting for transfers between devices  83 us (37%)
  blocking collectives  65.6 us (30%)
  local copies, waits for them, and re-layouts  31.6 us (14%)
  other arithmetic  17.5 us (8%)
  between operations  13.5 us (6%)
  matrix products  9.93 us (4%)
    reduce_scatter x1, waiting for transfers between devices, per_device(): lax.psum_scatter(product.reshape(degrees, own_slots * columns), 'lat', sc...  83 us
    all_to_all x1, blocking collectives, per_device(): lax.all_to_all(ordered, 'wave', split_axis=1, concat_axis=0, tiled=True)  65.6 us
    reshape x1, local copies, waits for them, and re-layouts, per_device(): product.reshape(degrees, own_slots * columns)  11.4 us
    dot_general x1, matrix products, per_device(): jnp.einsum('sjn,jsc->nsc', table, weighted, preferred_element_type=jnp.fl...  9.93 us
    gather x3, local copies, waits for them, and re-layouts, per_device(): jnp.take(spread, owner_order, axis=1)  9.55 us
    convert_element_type x1, local copies, waits for them, and re-layouts, per_device(): band_rows.astype(jnp.float32)  7.56 us
  transfers between devices with their start and end apart: 1, of which 1 were waited for; matrix products, arithmetic and copies ran while one was open for 0% of the time, Pallas kernels for 0%

commit v1 on v0

--- a/solution.py
+++ b/solution.py
@@ -1,10 +1,21 @@
+import functools
+
 import jax
 import jax.numpy as jnp
 from jax import lax
+from jax.experimental import pallas as pl
+from jax.experimental.pallas import tpu as pltpu
 from jax.sharding import PartitionSpec as P
 
-
-def per_device(fourier, row_points, owner_order, gauss_weight, table):
+WHOLE = pl.BlockSpec(memory_space=pltpu.VMEM)
+SCALARS = pl.BlockSpec(memory_space=pltpu.SMEM)
+PARAMS = pltpu.CompilerParams(vmem_limit_bytes=48 * 2**20)
+SMALL = pl.CostEstimate(flops=1, transcendentals=0, bytes_accessed=1)
+WINDOW = 3
+CUTS = ((0, 0, 4), (1, 0, 4), (2, 0, 4), (3, 0, 3), (3, 3, 1))
+
+
+def plain(fourier, row_points, owner_order, gauss_weight, table):
     slot_total = owner_order.shape[0]
     own_slots, band_count, degrees = table.shape
     stride = degrees // slot_total
@@ -35,6 +46,253 @@
     return result.reshape(share, own_slots * columns)
 
 
+def exchange(value, axis, step):
+    size = lax.axis_size(axis)
+    with jax.named_scope(f"{axis}_{step}"):
+        return lax.ppermute(value, axis, [(i, i ^ step) for i in range(size)])
+
+
+def after(value, *earlier):
+    return lax.optimization_barrier((value, *earlier))[0]
+
+
+def prepare_body(stride, own_slots, chunks, owner_hbm, gauss_hbm, points_hbm, source, *refs):
+    count = 4 * len(chunks)
+    results, landed = refs[:count], refs[count : 2 * count]
+    owner_ref, gauss_ref, points_ref, sems = refs[2 * count :]
+    rows = points_ref.shape[0]
+    band = gauss_ref.shape[0]
+    columns = source.shape[1] // owner_ref.shape[0]
+    wave = lax.axis_index("wave")
+
+    copies = [
+        pltpu.make_async_copy(gauss_hbm, gauss_ref, sems.at[count]),
+        pltpu.make_async_copy(points_hbm, points_ref, sems.at[count + 1]),
+    ]
+    owners = pltpu.make_async_copy(owner_hbm, owner_ref, sems.at[count + 2])
+    for copy in (owners, *copies):
+        copy.start()
+    owners.wait()
+    kinds = []
+    for at, (slot, offset, width) in enumerate(chunks):
+        for step in range(4):
+            kind = owner_ref[(wave ^ step) * own_slots + slot]
+            start = pl.multiple_of(kind * columns + offset, 128)
+            kinds.append(kind)
+            copies.append(
+                pltpu.make_async_copy(
+                    source.at[:, pl.ds(start, width)],
+                    landed[4 * at + step],
+                    sems.at[4 * at + step],
+                )
+            )
+    for copy in copies[2:]:
+        copy.start()
+    copies[0].wait()
+    copies[1].wait()
+    row = lax.broadcasted_iota(jnp.int32, (rows, band), 0)
+    lane = lax.broadcasted_iota(jnp.int32, (rows, band), 1)
+    weight = jnp.sum(
+        jnp.where(lane == row + wave * rows, gauss_ref[...][None, :], 0.0), axis=1, keepdims=True
+    )
+    row = lax.broadcasted_iota(jnp.int32, (rows, rows), 0)
+    lane = lax.broadcasted_iota(jnp.int32, (rows, rows), 1)
+    points = jnp.sum(
+        jnp.where(lane == row, points_ref[...].astype(jnp.float32)[None, :], 0.0),
+        axis=1,
+        keepdims=True,
+    )
+    for at in range(count):
+        copies[2 + at].wait()
+        kept = points >= (2 * kinds[at] * stride + 2).astype(jnp.float32)
+        value = jnp.where(kept, landed[at][...].astype(jnp.float32) * weight, 0.0)
+        results[at][...] = value.astype(jnp.bfloat16)
+
+
+def prepare(fourier, row_points, owner_order, gauss_weight, own_slots, stride, chunks):
+    rows = fourier.shape[0]
+    blocks = [(rows, width) for _, _, width in chunks for _ in range(4)]
+    hbm = pl.BlockSpec(memory_space=pltpu.HBM)
+    outs = pl.pallas_call(
+        functools.partial(prepare_body, stride, own_slots, chunks),
+        in_specs=[hbm] * 4,
+        out_specs=[WHOLE] * len(blocks),
+        out_shape=[jax.ShapeDtypeStruct(block, jnp.bfloat16) for block in blocks],
+        scratch_shapes=[pltpu.VMEM(block, jnp.bfloat16) for block in blocks]
+        + [
+            pltpu.SMEM(owner_order.shape, jnp.int32),
+            pltpu.VMEM(gauss_weight.shape, jnp.float32),
+            pltpu.VMEM(row_points.shape, jnp.int32),
+            pltpu.SemaphoreType.DMA((len(blocks) + 3,)),
+        ],
+        compiler_params=PARAMS,
+        cost_estimate=SMALL,
+        name="prepare",
+    )(
+        *[
+            pltpu.with_memory_space_constraint(array, pltpu.HBM)
+            for array in (owner_order, gauss_weight, row_points, fourier)
+        ],
+    )
+    return [list(outs[4 * at : 4 * at + 4]) for at in range(len(chunks))]
+
+
+def turn_body(rows, stride, owner_ref, table_ref, limit_ref, *outs):
+    wave = lax.axis_index("wave")
+    own_slots = len(outs)
+    for slot, out in enumerate(outs):
+        limit_ref[slot] = jnp.full(
+            limit_ref.shape[1:], owner_ref[wave * own_slots + slot] * stride, jnp.int32
+        )
+        for step in range(4):
+            start = pl.multiple_of((wave ^ step) * rows, 16)
+            out[:, step * rows : (step + 1) * rows] = table_ref[slot, pl.ds(start, rows), :].T
+
+
+def turn(owner_order, table, rows, stride, columns):
+    own_slots, band, degrees = table.shape
+    return pl.pallas_call(
+        functools.partial(turn_body, rows, stride),
+        in_specs=[SCALARS, WHOLE],
+        out_specs=[WHOLE] * (1 + own_slots),
+        out_shape=[jax.ShapeDtypeStruct((own_slots, 8, columns), jnp.int32)]
+        + [jax.ShapeDtypeStruct((degrees, band), table.dtype)] * own_slots,
+        compiler_params=PARAMS,
+        cost_estimate=SMALL,
+        name="turn",
+    )(owner_order, table)
+
+
+def multiply_body(other, table_ref, own, one, two, three, out_ref):
+    share = out_ref.shape[1]
+    core = lax.axis_index("lat") & 1
+    rows = jnp.concatenate([own[...], one[...], two[...], three[...]], axis=0)
+    for half in range(2):
+        start = pl.multiple_of((2 * half + (1 - core if other else core)) * share, 16)
+        out_ref[half] = jnp.dot(
+            table_ref[pl.ds(start, share), :], rows, preferred_element_type=jnp.float32
+        ).astype(out_ref.dtype)
+
+
+def multiply(turned, pieces, other):
+    width = pieces[0].shape[1]
+    share = turned.shape[0] // 4
+    return pl.pallas_call(
+        functools.partial(multiply_body, other),
+        in_specs=[WHOLE] * 5,
+        out_specs=WHOLE,
+        out_shape=jax.ShapeDtypeStruct(
+            (2, share, width), jnp.bfloat16 if other else jnp.float32
+        ),
+        compiler_params=PARAMS,
+        cost_estimate=SMALL,
+        name="multiply_other" if other else "multiply_own",
+    )(turned, *pieces)
+
+
+def combine_body(keep_ref, got_ref, send_ref):
+    near = 1 - (lax.axis_index("lat") >> 1)
+    send_ref[...] = (keep_ref[near] + got_ref[near].astype(jnp.float32)).astype(jnp.bfloat16)
+
+
+def combine(keep, got):
+    return pl.pallas_call(
+        combine_body,
+        in_specs=[WHOLE] * 2,
+        out_specs=WHOLE,
+        out_shape=jax.ShapeDtypeStruct(keep.shape[1:], jnp.bfloat16),
+        compiler_params=PARAMS,
+        cost_estimate=SMALL,
+        name="combine",
+    )(keep, got)
+
+
+def finish_body(slot, start, limit_ref, keep_ref, near_ref, far_ref, *refs):
+    out_ref, total_ref, sem = refs[-3:]
+    share, width = total_ref.shape
+    lat = lax.axis_index("lat")
+    far = lat >> 1
+    degree = lat * share + lax.broadcasted_iota(jnp.int32, (share, width), 0)
+    total = keep_ref[far] + near_ref[far].astype(jnp.float32) + far_ref[...].astype(jnp.float32)
+    total_ref[...] = jnp.where(degree >= limit_ref[slot, 0:1, :width], total, 0.0)
+    copy = pltpu.make_async_copy(total_ref, out_ref.at[:, start : start + width], sem)
+    copy.start()
+    copy.wait()
+
+
+def finish(limits, keep, near, far, before, chunk):
+    _, share, width = keep.shape
+    own_slots, _, columns = limits.shape
+    slot, offset, _ = chunk
+    old = [] if before is None else [before]
+    hbm = pl.BlockSpec(memory_space=pltpu.HBM)
+    return pl.pallas_call(
+        functools.partial(finish_body, slot, slot * columns + offset),
+        in_specs=[WHOLE] * 4 + [hbm] * len(old),
+        out_specs=hbm,
+        out_shape=pltpu.HBM((share, own_slots * columns), jnp.float32),
+        input_output_aliases={4: 0} if old else {},
+        scratch_shapes=[pltpu.VMEM((share, width), jnp.float32), pltpu.SemaphoreType.DMA],
+        compiler_params=PARAMS,
+        cost_estimate=SMALL,
+        name="finish",
+    )(limits, keep, near, far, *old)
+
+
+def piped(fourier, row_points, owner_order, gauss_weight, table):
+    slot_total = owner_order.shape[0]
+    own_slots, _, degrees = table.shape
+    stride = degrees // slot_total
+    columns = fourier.shape[1] // slot_total
+    chunks = [
+        (slot, first * columns // 4, parts * columns // 4) for slot, first, parts in CUTS
+    ]
+    count = len(chunks)
+    scalars = (fourier, row_points, owner_order, gauss_weight, own_slots, stride)
+    pieces = prepare(*scalars, chunks[:1])
+    arrived = [{0: piece[0]} for piece in pieces]
+    queue = [(0, 2), (0, 3)]
+    for at, step in queue + [(0, 1)]:
+        arrived[at][step] = exchange(pieces[at][step], "wave", step)
+    pieces += prepare(*scalars, chunks[1:])
+    arrived += [{0: piece[0]} for piece in pieces[1:]]
+    queue += [(at, step) for at in range(1, count) for step in (2, 3)]
+
+    def send(place, *earlier):
+        if place < len(queue):
+            at, step = queue[place]
+            if place >= WINDOW:
+                was, by = queue[place - WINDOW]
+                earlier = (*earlier, arrived[was][by])
+            arrived[at][step] = exchange(after(pieces[at][step], *earlier), "wave", step)
+
+    for place in range(2, WINDOW):
+        send(place)
+    limits, *turned = turn(
+        after(owner_order, pieces[1][0]), table, fourier.shape[0], stride, columns
+    )
+    token = limits
+    totals = pending = None
+    for at, chunk in enumerate(chunks):
+        if pending is not None:
+            token = totals = finish(limits, *pending, totals, chunks[at - 1])
+        for place in (2 * at + WINDOW, 2 * at + 1 + WINDOW):
+            send(place, token)
+        if at + 1 < count:
+            arrived[at + 1][1] = exchange(
+                after(pieces[at + 1][1], token, arrived[at][1]), "wave", 1
+            )
+        got = [arrived[at][step] for step in range(4)]
+        got[0] = after(got[0], token, *got[1:])
+        other = multiply(turned[chunk[0]], got, True)
+        near = exchange(other, "lat", 1)
+        got[0] = after(got[0], other)
+        keep = multiply(turned[chunk[0]], got, False)
+        token = sent = combine(keep, near)
+        pending = (keep, near, exchange(sent, "lat", 2))
+    return finish(limits, *pending, totals, chunks[-1])
+
+
 def solution(mesh):
     in_specs = (
         P(("grp", "lat", "wave"), None),
@@ -44,6 +302,19 @@
         P("wave", "lat", None),
     )
     out_specs = P(("grp", "lat"), "wave")
+
+    def per_device(fourier, row_points, owner_order, gauss_weight, table):
+        columns = fourier.shape[1] // owner_order.shape[0]
+        four = mesh.shape["wave"] == 4 and mesh.shape["lat"] == 4
+        whole = (
+            table.shape[0] == 4
+            and fourier.shape[0] % 16 == 0
+            and (table.shape[2] // 4) % 16 == 0
+            and columns % 512 == 0
+        )
+        body = piped if four and whole else plain
+        return body(fourier, row_points, owner_order, gauss_weight, table)
+
     return jax.shard_map(
         per_device, mesh=mesh, in_specs=in_specs, out_specs=out_specs, check_vma=False
     )

time: 222 us -> 97.1 us (0.44)
  blocking collectives: 65.6 us -> 0 us
  waiting for transfers between devices: 83 us -> 41.2 us
  local copies, waits for them, and re-layouts: 31.6 us -> 0.01 us
  starting transfers between devices: 0.01 us -> 31.1 us
  Pallas kernels: 0 us -> 24.2 us
  other arithmetic: 17.5 us -> 0 us
  between operations: 13.5 us -> 0.23 us
  matrix products: 9.93 us -> 0 us
    reduce_scatter x1 -> x0, waiting for transfers between devices: 83 us -> none  [per_device(): lax.psum_scatter(product.reshape(degrees, own_slots * columns), 'lat', sc...]
    all_to_all x1 -> x0, blocking collectives: 65.6 us -> none  [per_device(): lax.all_to_all(ordered, 'wave', split_axis=1, concat_axis=0, tiled=True)]
    ppermute x0 -> x25, waiting for transfers between devices: none -> 41.2 us  [exchange(): return lax.ppermute(value, axis, [(i, i ^ step) for i in range(size)])]
    ppermute x0 -> x25, starting transfers between devices: none -> 31.1 us  [exchange(): return lax.ppermute(value, axis, [(i, i ^ step) for i in range(size)])]
    pallas_call x0 -> x23, Pallas kernels: none -> 24.2 us  [the longest x1 8.9 us: turn(): pl.pallas_call(functools.partial(turn_body, rows, stride), in_specs=[SCAL...]
    reshape x1 -> x0, local copies, waits for them, and re-layouts: 11.4 us -> none  [per_device(): product.reshape(degrees, own_slots * columns)]
    dot_general x1 -> x0, matrix products: 9.93 us -> none  [per_device(): jnp.einsum('sjn,jsc->nsc', table, weighted, preferred_element_type=jnp.fl...]
    gather x3 -> x0, local copies, waits for them, and re-layouts: 9.55 us -> none  [per_device(): jnp.take(spread, owner_order, axis=1)]
  transfers between devices with their start and end apart: 1 -> 25, of which waited for: 1 -> 17; matrix products, arithmetic and copies ran while one was open for 0% -> 0% of each run, Pallas kernels for 0% -> 19%
where the time goes in v1:
time: 97.1 us; the launch traced here: 96.8 us
  waiting for transfers between devices  41.2 us (42%)
  starting transfers between devices  31.1 us (32%)
  Pallas kernels  24.2 us (25%)
    ppermute x25, waiting for transfers between devices, exchange(): return lax.ppermute(value, axis, [(i, i ^ step) for i in range(size)])  41.2 us
    ppermute x25, starting transfers between devices, exchange(): return lax.ppermute(value, axis, [(i, i ^ step) for i in range(size)])  31.1 us
    pallas_call x1, Pallas kernels, turn(): pl.pallas_call(functools.partial(turn_body, rows, stride), in_specs=[SCAL...  8.9 us
    pallas_call x10, Pallas kernels, multiply(): pl.pallas_call(functools.partial(multiply_body, other), in_specs=[WHOLE]...  6 us
    pallas_call x5, Pallas kernels, finish(): pl.pallas_call(functools.partial(finish_body, slot, slot * columns + offs...  4.58 us
    pallas_call x2, Pallas kernels, prepare(): pl.pallas_call(functools.partial(prepare_body, stride, own_slots, chunks)...  4.54 us
  transfers between devices with their start and end apart: 25, of which 17 were waited for; matrix products, arithmetic and copies ran while one was open for 0% of the time, Pallas kernels for 19%

profile of v1, /device:TPU:0, one launch (start us, length us, event | category | flops | bytes accessed | tf_op | source)
XLA Modules:
  0.0 96.8 jit_solution(6879142154721714574)
XLA Ops:
  0.0 2.1 %prepare.3 = (bf16[160,512]{1,0:T(8,128)(2,1)S(1)}, bf16[160,512]{1,0:T(8,128)(2,1)S(1)}, bf16[160,512]{1,0:T(8,128)(2,1)S(1)}, bf16[160,512]{1,0:T(8,128)(2,1)S(1)}) custom-call(s32[16]{0:T(128)} %owner_hbm.3, f32[640]{0:T(1024)} %gauss_hbm.3, s32[160]{0:T(256)} %points_hbm.3, bf16[160,8192]{1,0:T(8,128)(2,1)} %source.3), custom_call_target="tpu_custom_call" | custom-call | flops 1 | bytes 1 | tf_op jit(solution)/shard_map/prepare/pallas_call | solution.py:116
  2.1 3.1 %collective-permute-start = (bf16[160,512]{1,0:T(8,128)(2,1)S(1)}, bf16[160,512]{1,0:T(8,128)(2,1)S(1)}, u32[]{:S(2)}, u32[]{:S(2)}) collective-permute-start(bf16[160,512]{1,0:T(8,128)(2,1)S(1)} %get-tuple-element.63), channel_id=1, source_target_pairs={{0,4},{4,0},{8,12},{12,8},{1,5},{5,1},{9,13},{13,9},{2,6},{6,2},{1... | collective-permute-start | bytes 491528 | tf_op jit(solution)/shard_map/wave_1/ppermute | solution.py:52
  5.2 2.6 %collective-permute-start.1 = (bf16[160,512]{1,0:T(8,128)(2,1)S(1)}, bf16[160,512]{1,0:T(8,128)(2,1)S(1)}, u32[]{:S(2)}, u32[]{:S(2)}) collective-permute-start(bf16[160,512]{1,0:T(8,128)(2,1)S(1)} %get-tuple-element.64), channel_id=1, source_target_pairs={{0,8},{4,12},{8,0},{12,4},{1,9},{5,13},{9,1},{13,5},{2,10},{6,14},... | collective-permute-start | bytes 491528 | tf_op jit(solution)/shard_map/wave_2/ppermute | solution.py:52
  7.8 2.5 %prepare.2 = (bf16[160,512]{1,0:T(8,128)(2,1)S(1)}, bf16[160,512]{1,0:T(8,128)(2,1)S(1)}, bf16[160,512]{1,0:T(8,128)(2,1)S(1)}, bf16[160,512]{1,0:T(8,128)(2,1)S...) custom-call(s32[16]{0:T(128)} %owner_hbm.3, ...), custom_call_target="tpu_custom_call" | custom-call | flops 1 | bytes 1 | tf_op jit(solution)/shard_map/prepare/pallas_call | solution.py:116
  10.2 8.9 %turn.1 = (s32[4,8,512]{2,1,0:T(8,128)S(1)}, bf16[1280,640]{1,0:T(8,128)(2,1)S(1)}, bf16[1280,640]{1,0:T(8,128)(2,1)S(1)}, bf16[1280,640]{1,0:T(8,128)(2,1)S(1)}, bf16[1280,640]{1,0:T(8,128)(2,1)}) custom-call(s32[16]{0:T(128)S(1)} %copy-done.1, bf16[4,640,1280]{2,1,0:T(8,128)(2,1)} %table_ref.1), custom_call_target="tpu_custom_call" | custom-call | flops 1 | bytes 1 | tf_op jit(solution)/shard_map/turn/pallas_call | solution.py:154
  23.1 1.6 %collective-permute-start.4 = (bf16[320,512]{1,0:T(8,128)(2,1)S(1)}, bf16[320,512]{1,0:T(8,128)(2,1)S(1)}, u32[]{:S(2)}, u32[]{:S(2)}) collective-permute-start(bf16[320,512]{1,0:T(8,128)(2,1)S(1)} %combine.5), channel_id=1, source_target_pairs={{0,2},{1,3},{2,0},{3,1},{4,6},{5,7},{6,4},{7,5},{8,10},{9,11},{10,... | collective-permute-start | bytes 983048 | tf_op jit(solution)/shard_map/lat_2/ppermute | solution.py:52
  24.7 3.7 %collective-permute-start.6 = (bf16[160,512]{1,0:T(8,128)(2,1)S(1)}, bf16[160,512]{1,0:T(8,128)(2,1)S(1)}, u32[]{:S(2)}, u32[]{:S(2)}) collective-permute-start(bf16[160,512]{1,0:T(8,128)(2,1)S(1)} %get-tuple-element.70), channel_id=1, source_target_pairs={{0,8},{4,12},{8,0},{12,4},{1,9},{5,13},{9,1},{13,5},{2,10},{6,14},... | collective-permute-start | bytes 491528 | tf_op jit(solution)/shard_map/wave_2/ppermute | solution.py:52
  29.8 3.1 %collective-permute-done.4.far_ref = bf16[320,512]{1,0:T(8,128)(2,1)S(1)} collective-permute-done((bf16[320,512]{1,0:T(8,128)(2,1)S(1)}, bf16[320,512]{1,0:T(8,128)(2,1)S(1)}, u32[]{:S(2)}, u32[]{:S(2)}) %collective-permute-start.4) | collective-permute-done | bytes 327712 | tf_op jit(solution)/shard_map/lat_2/ppermute | solution.py:52
  33.9 3.7 %collective-permute-done.6.two = bf16[160,512]{1,0:T(8,128)(2,1)S(1)} collective-permute-done((bf16[160,512]{1,0:T(8,128)(2,1)S(1)}, bf16[160,512]{1,0:T(8,128)(2,1)S(1)}, u32[]{:S(2)}, u32[]{:S(2)}) %collective-permute-start.6) | collective-permute-done | bytes 163872 | tf_op jit(solution)/shard_map/wave_2/ppermute | solution.py:52
  37.6 3.2 %collective-permute-done.7.three = bf16[160,512]{1,0:T(8,128)(2,1)S(1)} collective-permute-done((bf16[160,512]{1,0:T(8,128)(2,1)S(1)}, bf16[160,512]{1,0:T(8,128)(2,1)S(1)}, u32[]{:S(2)}, u32[]{:S(2)}) %collective-permute-start.7) | collective-permute-done | bytes 163872 | tf_op jit(solution)/shard_map/wave_3/ppermute | solution.py:52
  44.3 3.1 %collective-permute-start.11 = (bf16[160,512]{1,0:T(8,128)(2,1)S(1)}, bf16[160,512]{1,0:T(8,128)(2,1)S(1)}, u32[]{:S(2)}, u32[]{:S(2)}) collective-permute-start(bf16[160,512]{1,0:T(8,128)(2,1)S(1)} %get-tuple-element.78), channel_id=1, source_target_pairs={{0,8},{4,12},{8,0},{12,4},{1,9},{5,13},{9,1},{13,5},{2,10},{6,14},... | collective-permute-start | bytes 491528 | tf_op jit(solution)/shard_map/wave_2/ppermute | solution.py:52
  47.4 2.1 %collective-permute-start.12 = (bf16[160,512]{1,0:T(8,128)(2,1)S(1)}, bf16[160,512]{1,0:T(8,128)(2,1)S(1)}, u32[]{:S(2)}, u32[]{:S(2)}) collective-permute-start(bf16[160,512]{1,0:T(8,128)(2,1)S(1)} %get-tuple-element.80), channel_id=1, source_target_pairs={{0,12},{4,8},{8,4},{12,0},{1,13},{5,9},{9,5},{13,1},{2,14},{6,10},... | collective-permute-start | bytes 491528 | tf_op jit(solution)/shard_map/wave_3/ppermute | solution.py:52
  49.5 4.0 %collective-permute-done.9.far_ref = bf16[320,512]{1,0:T(8,128)(2,1)S(1)} collective-permute-done((bf16[320,512]{1,0:T(8,128)(2,1)S(1)}, bf16[320,512]{1,0:T(8,128)(2,1)S(1)}, u32[]{:S(2)}, u32[]{:S(2)}) %collective-permute-start.9) | collective-permute-done | bytes 327712 | tf_op jit(solution)/shard_map/lat_2/ppermute | solution.py:52
  56.0 4.6 %collective-permute-done.12.three = bf16[160,512]{1,0:T(8,128)(2,1)S(1)} collective-permute-done((bf16[160,512]{1,0:T(8,128)(2,1)S(1)}, bf16[160,512]{1,0:T(8,128)(2,1)S(1)}, u32[]{:S(2)}, u32[]{:S(2)}) %collective-permute-start.12) | collective-permute-done | bytes 163872 | tf_op jit(solution)/shard_map/wave_3/ppermute | solution.py:52
  63.5 1.6 %collective-permute-start.14 = (bf16[320,512]{1,0:T(8,128)(2,1)S(1)}, bf16[320,512]{1,0:T(8,128)(2,1)S(1)}, u32[]{:S(2)}, u32[]{:S(2)}) collective-permute-start(bf16[320,512]{1,0:T(8,128)(2,1)S(1)} %combine.7), channel_id=1, source_target_pairs={{0,2},{1,3},{2,0},{3,1},{4,6},{5,7},{6,4},{7,5},{8,10},{9,11},{10,... | collective-permute-start | bytes 983048 | tf_op jit(solution)/shard_map/lat_2/ppermute | solution.py:52
  65.1 2.7 %collective-permute-start.16 = (bf16[160,384]{1,0:T(8,128)(2,1)S(1)}, bf16[160,384]{1,0:T(8,128)(2,1)S(1)}, u32[]{:S(2)}, u32[]{:S(2)}) collective-permute-start(bf16[160,384]{1,0:T(8,128)(2,1)S(1)} %get-tuple-element.86), channel_id=1, source_target_pairs={{0,8},{4,12},{8,0},{12,4},{1,9},{5,13},{9,1},{13,5},{2,10},{6,14},... | collective-permute-start | bytes 368648 | tf_op jit(solution)/shard_map/wave_2/ppermute | solution.py:52
  67.8 1.8 %collective-permute-start.17 = (bf16[160,384]{1,0:T(8,128)(2,1)S(1)}, bf16[160,384]{1,0:T(8,128)(2,1)S(1)}, u32[]{:S(2)}, u32[]{:S(2)}) collective-permute-start(bf16[160,384]{1,0:T(8,128)(2,1)S(1)} %get-tuple-element.88), channel_id=1, source_target_pairs={{0,12},{4,8},{8,4},{12,0},{1,13},{5,9},{9,5},{13,1},{2,14},{6,10},... | collective-permute-start | bytes 368648 | tf_op jit(solution)/shard_map/wave_3/ppermute | solution.py:52
  69.6 3.8 %collective-permute-done.14.far_ref = bf16[320,512]{1,0:T(8,128)(2,1)S(1)} collective-permute-done((bf16[320,512]{1,0:T(8,128)(2,1)S(1)}, bf16[320,512]{1,0:T(8,128)(2,1)S(1)}, u32[]{:S(2)}, u32[]{:S(2)}) %collective-permute-start.14) | collective-permute-done | bytes 327712 | tf_op jit(solution)/shard_map/lat_2/ppermute | solution.py:52
  75.4 2.7 %collective-permute-done.17.three = bf16[160,384]{1,0:T(8,128)(2,1)S(1)} collective-permute-done((bf16[160,384]{1,0:T(8,128)(2,1)S(1)}, bf16[160,384]{1,0:T(8,128)(2,1)S(1)}, u32[]{:S(2)}, u32[]{:S(2)}) %collective-permute-start.17) | collective-permute-done | bytes 122912 | tf_op jit(solution)/shard_map/wave_3/ppermute | solution.py:52
  81.3 1.9 %collective-permute-start.21 = (bf16[160,128]{1,0:T(8,128)(2,1)S(1)}, bf16[160,128]{1,0:T(8,128)(2,1)S(1)}, u32[]{:S(2)}, u32[]{:S(2)}) collective-permute-start(bf16[160,128]{1,0:T(8,128)(2,1)S(1)} %get-tuple-element.94), channel_id=1, source_target_pairs={{0,8},{4,12},{8,0},{12,4},{1,9},{5,13},{9,1},{13,5},{2,10},{6,14},... | collective-permute-start | bytes 122888 | tf_op jit(solution)/shard_map/wave_2/ppermute | solution.py:52
  83.9 1.8 %collective-permute-start.22 = (bf16[160,128]{1,0:T(8,128)(2,1)S(1)}, bf16[160,128]{1,0:T(8,128)(2,1)S(1)}, u32[]{:S(2)}, u32[]{:S(2)}) collective-permute-start(bf16[160,128]{1,0:T(8,128)(2,1)S(1)} %get-tuple-element.96), channel_id=1, source_target_pairs={{0,12},{4,8},{8,4},{12,0},{1,13},{5,9},{9,5},{13,1},{2,14},{6,10},... | collective-permute-start | bytes 122888 | tf_op jit(solution)/shard_map/wave_3/ppermute | solution.py:52
  85.7 3.1 %collective-permute-done.19.far_ref = bf16[320,384]{1,0:T(8,128)(2,1)S(1)} collective-permute-done((bf16[320,384]{1,0:T(8,128)(2,1)S(1)}, bf16[320,384]{1,0:T(8,128)(2,1)S(1)}, u32[]{:S(2)}, u32[]{:S(2)}) %collective-permute-start.19) | collective-permute-done | bytes 245792 | tf_op jit(solution)/shard_map/lat_2/ppermute | solution.py:52
  91.5 1.6 %collective-permute-start.24 = (bf16[320,128]{1,0:T(8,128)(2,1)S(1)}, bf16[320,128]{1,0:T(8,128)(2,1)S(1)}, u32[]{:S(2)}, u32[]{:S(2)}) collective-permute-start(bf16[320,128]{1,0:T(8,128)(2,1)S(1)} %combine.9), channel_id=1, source_target_pairs={{0,2},{1,3},{2,0},{3,1},{4,6},{5,7},{6,4},{7,5},{8,10},{9,11},{10,... | collective-permute-start | bytes 245768 | tf_op jit(solution)/shard_map/lat_2/ppermute | solution.py:52
  93.1 3.0 %collective-permute-done.24.far_ref = bf16[320,128]{1,0:T(8,128)(2,1)S(1)} collective-permute-done((bf16[320,128]{1,0:T(8,128)(2,1)S(1)}, bf16[320,128]{1,0:T(8,128)(2,1)S(1)}, u32[]{:S(2)}, u32[]{:S(2)}) %collective-permute-start.24) | collective-permute-done | bytes 81952 | tf_op jit(solution)/shard_map/lat_2/ppermute | solution.py:52
  (53 shorter events, 24.7 us)
Async XLA Ops:
  2.1 17.1 %collective-permute-start = (bf16[160,512]{1,0:T(8,128)(2,1)S(1)}, bf16[160,512]{1,0:T(8,128)(2,1)S(1)}, u32[]{:S(2)}, u32[]{:S(2)}) collective-permute-start(bf16[160,512]{1,0:T(8,128)(2,1)S(1)} %get-tuple-element.63), channel_id=1, source_target_pairs={{0,4},{4,0},{8,12},{12,8},{1,5},{5,1},{9,13},{13,9},{2,6},{6,2},{1... | collective-permute-start | bytes 491528 | tf_op jit(solution)/shard_map/wave_1/ppermute | solution.py:52
  5.2 15.0 %collective-permute-start.1 = (bf16[160,512]{1,0:T(8,128)(2,1)S(1)}, bf16[160,512]{1,0:T(8,128)(2,1)S(1)}, u32[]{:S(2)}, u32[]{:S(2)}) collective-permute-start(bf16[160,512]{1,0:T(8,128)(2,1)S(1)} %get-tuple-element.64), channel_id=1, source_target_pairs={{0,8},{4,12},{8,0},{12,4},{1,9},{5,13},{9,1},{13,5},{2,10},{6,14},... | collective-permute-start | bytes 491528 | tf_op jit(solution)/shard_map/wave_2/ppermute | solution.py:52
  7.7 12.5 %collective-permute-start.2 = (bf16[160,512]{1,0:T(8,128)(2,1)S(1)}, bf16[160,512]{1,0:T(8,128)(2,1)S(1)}, u32[]{:S(2)}, u32[]{:S(2)}) collective-permute-start(bf16[160,512]{1,0:T(8,128)(2,1)S(1)} %get-tuple-element.65), channel_id=1, source_target_pairs={{0,12},{4,8},{8,4},{12,0},{1,13},{5,9},{9,5},{13,1},{2,14},{6,10},... | collective-permute-start | bytes 491528 | tf_op jit(solution)/shard_map/wave_3/ppermute | solution.py:52
  20.9 2.2 %collective-permute-start.3 = (bf16[2,320,512]{2,1,0:T(8,128)(2,1)S(1)}, bf16[2,320,512]{2,1,0:T(8,128)(2,1)S(1)}, u32[]{:S(2)}, u32[]{:S(2)}) collective-permute-start(bf16[2,320,512]{2,1,0:T(8,128)(2,1)S(1)} %multiply_other.5), channel_id=1, source_target_pairs={{0,1},{1,0},{2,3},{3,2},{4,5},{5,4},{6,7},{7,6},{8,9},{9,8},{10,11... | collective-permute-start | bytes 1966088 | tf_op jit(solution)/shard_map/lat_1/ppermute | solution.py:52
  23.1 9.8 %collective-permute-start.4 = (bf16[320,512]{1,0:T(8,128)(2,1)S(1)}, bf16[320,512]{1,0:T(8,128)(2,1)S(1)}, u32[]{:S(2)}, u32[]{:S(2)}) collective-permute-start(bf16[320,512]{1,0:T(8,128)(2,1)S(1)} %combine.5), channel_id=1, source_target_pairs={{0,2},{1,3},{2,0},{3,1},{4,6},{5,7},{6,4},{7,5},{8,10},{9,11},{10,... | collective-permute-start | bytes 983048 | tf_op jit(solution)/shard_map/lat_2/ppermute | solution.py:52
  24.7 13.0 %collective-permute-start.6 = (bf16[160,512]{1,0:T(8,128)(2,1)S(1)}, bf16[160,512]{1,0:T(8,128)(2,1)S(1)}, u32[]{:S(2)}, u32[]{:S(2)}) collective-permute-start(bf16[160,512]{1,0:T(8,128)(2,1)S(1)} %get-tuple-element.70), channel_id=1, source_target_pairs={{0,8},{4,12},{8,0},{12,4},{1,9},{5,13},{9,1},{13,5},{2,10},{6,14},... | collective-permute-start | bytes 491528 | tf_op jit(solution)/shard_map/wave_2/ppermute | solution.py:52
  28.3 9.3 %collective-permute-start.5 = (bf16[160,512]{1,0:T(8,128)(2,1)S(1)}, bf16[160,512]{1,0:T(8,128)(2,1)S(1)}, u32[]{:S(2)}, u32[]{:S(2)}) collective-permute-start(bf16[160,512]{1,0:T(8,128)(2,1)S(1)} %get-tuple-element.69), channel_id=1, source_target_pairs={{0,4},{4,0},{8,12},{12,8},{1,5},{5,1},{9,13},{13,9},{2,6},{6,2},{1... | collective-permute-start | bytes 491528 | tf_op jit(solution)/shard_map/wave_1/ppermute | solution.py:52
  28.3 12.5 %collective-permute-start.7 = (bf16[160,512]{1,0:T(8,128)(2,1)S(1)}, bf16[160,512]{1,0:T(8,128)(2,1)S(1)}, u32[]{:S(2)}, u32[]{:S(2)}) collective-permute-start(bf16[160,512]{1,0:T(8,128)(2,1)S(1)} %get-tuple-element.72), channel_id=1, source_target_pairs={{0,12},{4,8},{8,4},{12,0},{1,13},{5,9},{9,5},{13,1},{2,14},{6,10},... | collective-permute-start | bytes 491528 | tf_op jit(solution)/shard_map/wave_3/ppermute | solution.py:52
  41.5 2.2 %collective-permute-start.8 = (bf16[2,320,512]{2,1,0:T(8,128)(2,1)S(1)}, bf16[2,320,512]{2,1,0:T(8,128)(2,1)S(1)}, u32[]{:S(2)}, u32[]{:S(2)}) collective-permute-start(bf16[2,320,512]{2,1,0:T(8,128)(2,1)S(1)} %multiply_other.6), channel_id=1, source_target_pairs={{0,1},{1,0},{2,3},{3,2},{4,5},{5,4},{6,7},{7,6},{8,9},{9,8},{10,11... | collective-permute-start | bytes 1966088 | tf_op jit(solution)/shard_map/lat_1/ppermute | solution.py:52
  43.7 9.8 %collective-permute-start.9 = (bf16[320,512]{1,0:T(8,128)(2,1)S(1)}, bf16[320,512]{1,0:T(8,128)(2,1)S(1)}, u32[]{:S(2)}, u32[]{:S(2)}) collective-permute-start(bf16[320,512]{1,0:T(8,128)(2,1)S(1)} %combine.6), channel_id=1, source_target_pairs={{0,2},{1,3},{2,0},{3,1},{4,6},{5,7},{6,4},{7,5},{8,10},{9,11},{10,... | collective-permute-start | bytes 983048 | tf_op jit(solution)/shard_map/lat_2/ppermute | solution.py:52
  44.3 11.7 %collective-permute-start.11 = (bf16[160,512]{1,0:T(8,128)(2,1)S(1)}, bf16[160,512]{1,0:T(8,128)(2,1)S(1)}, u32[]{:S(2)}, u32[]{:S(2)}) collective-permute-start(bf16[160,512]{1,0:T(8,128)(2,1)S(1)} %get-tuple-element.78), channel_id=1, source_target_pairs={{0,8},{4,12},{8,0},{12,4},{1,9},{5,13},{9,1},{13,5},{2,10},{6,14},... | collective-permute-start | bytes 491528 | tf_op jit(solution)/shard_map/wave_2/ppermute | solution.py:52
  47.4 8.6 %collective-permute-start.10 = (bf16[160,512]{1,0:T(8,128)(2,1)S(1)}, bf16[160,512]{1,0:T(8,128)(2,1)S(1)}, u32[]{:S(2)}, u32[]{:S(2)}) collective-permute-start(bf16[160,512]{1,0:T(8,128)(2,1)S(1)} %get-tuple-element.76), channel_id=1, source_target_pairs={{0,4},{4,0},{8,12},{12,8},{1,5},{5,1},{9,13},{13,9},{2,6},{6,2},{1... | collective-permute-start | bytes 491528 | tf_op jit(solution)/shard_map/wave_1/ppermute | solution.py:52
  47.4 13.2 %collective-permute-start.12 = (bf16[160,512]{1,0:T(8,128)(2,1)S(1)}, bf16[160,512]{1,0:T(8,128)(2,1)S(1)}, u32[]{:S(2)}, u32[]{:S(2)}) collective-permute-start(bf16[160,512]{1,0:T(8,128)(2,1)S(1)} %get-tuple-element.80), channel_id=1, source_target_pairs={{0,12},{4,8},{8,4},{12,0},{1,13},{5,9},{9,5},{13,1},{2,14},{6,10},... | collective-permute-start | bytes 491528 | tf_op jit(solution)/shard_map/wave_3/ppermute | solution.py:52
  61.3 2.2 %collective-permute-start.13 = (bf16[2,320,512]{2,1,0:T(8,128)(2,1)S(1)}, bf16[2,320,512]{2,1,0:T(8,128)(2,1)S(1)}, u32[]{:S(2)}, u32[]{:S(2)}) collective-permute-start(bf16[2,320,512]{2,1,0:T(8,128)(2,1)S(1)} %multiply_other.7), channel_id=1, source_target_pairs={{0,1},{1,0},{2,3},{3,2},{4,5},{5,4},{6,7},{7,6},{8,9},{9,8},{10,11... | collective-permute-start | bytes 1966088 | tf_op jit(solution)/shard_map/lat_1/ppermute | solution.py:52
  63.5 9.8 %collective-permute-start.14 = (bf16[320,512]{1,0:T(8,128)(2,1)S(1)}, bf16[320,512]{1,0:T(8,128)(2,1)S(1)}, u32[]{:S(2)}, u32[]{:S(2)}) collective-permute-start(bf16[320,512]{1,0:T(8,128)(2,1)S(1)} %combine.7), channel_id=1, source_target_pairs={{0,2},{1,3},{2,0},{3,1},{4,6},{5,7},{6,4},{7,5},{8,10},{9,11},{10,... | collective-permute-start | bytes 983048 | tf_op jit(solution)/shard_map/lat_2/ppermute | solution.py:52
  65.1 10.3 %collective-permute-start.16 = (bf16[160,384]{1,0:T(8,128)(2,1)S(1)}, bf16[160,384]{1,0:T(8,128)(2,1)S(1)}, u32[]{:S(2)}, u32[]{:S(2)}) collective-permute-start(bf16[160,384]{1,0:T(8,128)(2,1)S(1)} %get-tuple-element.86), channel_id=1, source_target_pairs={{0,8},{4,12},{8,0},{12,4},{1,9},{5,13},{9,1},{13,5},{2,10},{6,14},... | collective-permute-start | bytes 368648 | tf_op jit(solution)/shard_map/wave_2/ppermute | solution.py:52
  67.8 7.6 %collective-permute-start.15 = (bf16[160,384]{1,0:T(8,128)(2,1)S(1)}, bf16[160,384]{1,0:T(8,128)(2,1)S(1)}, u32[]{:S(2)}, u32[]{:S(2)}) collective-permute-start(bf16[160,384]{1,0:T(8,128)(2,1)S(1)} %get-tuple-element.84), channel_id=1, source_target_pairs={{0,4},{4,0},{8,12},{12,8},{1,5},{5,1},{9,13},{13,9},{2,6},{6,2},{1... | collective-permute-start | bytes 368648 | tf_op jit(solution)/shard_map/wave_1/ppermute | solution.py:52
  67.8 10.2 %collective-permute-start.17 = (bf16[160,384]{1,0:T(8,128)(2,1)S(1)}, bf16[160,384]{1,0:T(8,128)(2,1)S(1)}, u32[]{:S(2)}, u32[]{:S(2)}) collective-permute-start(bf16[160,384]{1,0:T(8,128)(2,1)S(1)} %get-tuple-element.88), channel_id=1, source_target_pairs={{0,12},{4,8},{8,4},{12,0},{1,13},{5,9},{9,5},{13,1},{2,14},{6,10},... | collective-permute-start | bytes 368648 | tf_op jit(solution)/shard_map/wave_3/ppermute | solution.py:52
  78.7 1.9 %collective-permute-start.18 = (bf16[2,320,384]{2,1,0:T(8,128)(2,1)S(1)}, bf16[2,320,384]{2,1,0:T(8,128)(2,1)S(1)}, u32[]{:S(2)}, u32[]{:S(2)}) collective-permute-start(bf16[2,320,384]{2,1,0:T(8,128)(2,1)S(1)} %multiply_other.8), channel_id=1, source_target_pairs={{0,1},{1,0},{2,3},{3,2},{4,5},{5,4},{6,7},{7,6},{8,9},{9,8},{10,11... | collective-permute-start | bytes 1474568 | tf_op jit(solution)/shard_map/lat_1/ppermute | solution.py:52
  80.7 8.1 %collective-permute-start.19 = (bf16[320,384]{1,0:T(8,128)(2,1)S(1)}, bf16[320,384]{1,0:T(8,128)(2,1)S(1)}, u32[]{:S(2)}, u32[]{:S(2)}) collective-permute-start(bf16[320,384]{1,0:T(8,128)(2,1)S(1)} %combine.8), channel_id=1, source_target_pairs={{0,2},{1,3},{2,0},{3,1},{4,6},{5,7},{6,4},{7,5},{8,10},{9,11},{10,... | collective-permute-start | bytes 737288 | tf_op jit(solution)/shard_map/lat_2/ppermute | solution.py:52
  81.3 8.4 %collective-permute-start.21 = (bf16[160,128]{1,0:T(8,128)(2,1)S(1)}, bf16[160,128]{1,0:T(8,128)(2,1)S(1)}, u32[]{:S(2)}, u32[]{:S(2)}) collective-permute-start(bf16[160,128]{1,0:T(8,128)(2,1)S(1)} %get-tuple-element.94), channel_id=1, source_target_pairs={{0,8},{4,12},{8,0},{12,4},{1,9},{5,13},{9,1},{13,5},{2,10},{6,14},... | collective-permute-start | bytes 122888 | tf_op jit(solution)/shard_map/wave_2/ppermute | solution.py:52
  83.1 6.5 %collective-permute-start.20 = (bf16[160,128]{1,0:T(8,128)(2,1)S(1)}, bf16[160,128]{1,0:T(8,128)(2,1)S(1)}, u32[]{:S(2)}, u32[]{:S(2)}) collective-permute-start(bf16[160,128]{1,0:T(8,128)(2,1)S(1)} %get-tuple-element.92), channel_id=1, source_target_pairs={{0,4},{4,0},{8,12},{12,8},{1,5},{5,1},{9,13},{13,9},{2,6},{6,2},{1... | collective-permute-start | bytes 122888 | tf_op jit(solution)/shard_map/wave_1/ppermute | solution.py:52
  83.9 5.8 %collective-permute-start.22 = (bf16[160,128]{1,0:T(8,128)(2,1)S(1)}, bf16[160,128]{1,0:T(8,128)(2,1)S(1)}, u32[]{:S(2)}, u32[]{:S(2)}) collective-permute-start(bf16[160,128]{1,0:T(8,128)(2,1)S(1)} %get-tuple-element.96), channel_id=1, source_target_pairs={{0,12},{4,8},{8,4},{12,0},{1,13},{5,9},{9,5},{13,1},{2,14},{6,10},... | collective-permute-start | bytes 122888 | tf_op jit(solution)/shard_map/wave_3/ppermute | solution.py:52
  91.5 4.6 %collective-permute-start.24 = (bf16[320,128]{1,0:T(8,128)(2,1)S(1)}, bf16[320,128]{1,0:T(8,128)(2,1)S(1)}, u32[]{:S(2)}, u32[]{:S(2)}) collective-permute-start(bf16[320,128]{1,0:T(8,128)(2,1)S(1)} %combine.9), channel_id=1, source_target_pairs={{0,2},{1,3},{2,0},{3,1},{4,6},{5,7},{6,4},{7,5},{8,10},{9,11},{10,... | collective-permute-start | bytes 245768 | tf_op jit(solution)/shard_map/lat_2/ppermute | solution.py:52
  (3 other events, 20.2 us)

commit v2 on v0

--- a/solution.py
+++ b/solution.py
@@ -1,10 +1,24 @@
+import functools
+
 import jax
 import jax.numpy as jnp
 from jax import lax
+from jax.experimental import pallas as pl
+from jax.experimental.pallas import tpu as pltpu
 from jax.sharding import PartitionSpec as P
 
-
-def per_device(fourier, row_points, owner_order, gauss_weight, table):
+WHOLE = pl.BlockSpec(memory_space=pltpu.VMEM)
+SCALARS = pl.BlockSpec(memory_space=pltpu.SMEM)
+PARAMS = pltpu.CompilerParams(vmem_limit_bytes=48 * 2**20)
+LARGE = pl.CostEstimate(flops=20_000_000_000, transcendentals=0, bytes_accessed=1)
+SMALL = pl.CostEstimate(flops=1, transcendentals=0, bytes_accessed=1)
+WINDOW = 6
+EARLY = 2
+STEPS = (2, 3, 1)
+CUTS = (4, 8, 12, 14)
+
+
+def plain(fourier, row_points, owner_order, gauss_weight, table):
     slot_total = owner_order.shape[0]
     own_slots, band_count, degrees = table.shape
     stride = degrees // slot_total
@@ -35,6 +49,311 @@
     return result.reshape(share, own_slots * columns)
 
 
+def exchange(value, axis, step):
+    size = lax.axis_size(axis)
+    with jax.named_scope(f"{axis}_{step}"):
+        return lax.ppermute(value, axis, [(i, i ^ step) for i in range(size)])
+
+
+class Held(dict):
+    def tie(self, *names):
+        values = lax.optimization_barrier([self[name] for name in names])
+        self.update(zip(names, values))
+
+
+def units(first, last, columns):
+    found = []
+    for slot in range(first // columns, (last - 1) // columns + 1):
+        start, stop = max(first, slot * columns), min(last, (slot + 1) * columns)
+        found.append((slot, start - slot * columns, stop - start, start - first))
+    return found
+
+
+def prepare_body(stride, own_slots, chunks, masks, owner_hbm, gauss_hbm, points_hbm, source, *refs):
+    count = 4 * len(chunks)
+    results, landed = refs[:count], refs[count + masks : 2 * count + masks]
+    owner_ref, gauss_ref, points_ref, sems = refs[2 * count + masks :]
+    rows = points_ref.shape[0]
+    band = gauss_ref.shape[0]
+    columns = source.shape[1] // owner_ref.shape[0]
+    wave = lax.axis_index("wave")
+
+    small = [
+        pltpu.make_async_copy(owner_hbm, owner_ref, sems.at[0]),
+        pltpu.make_async_copy(gauss_hbm, gauss_ref, sems.at[1]),
+        pltpu.make_async_copy(points_hbm, points_ref, sems.at[2]),
+    ]
+    for copy in small:
+        copy.start()
+    small[0].wait()
+    blocks = []
+    for at, (first, last) in enumerate(chunks):
+        for step in STEPS + (0,):
+            for slot, offset, width, place in units(first, last, columns):
+                kind = owner_ref[(wave ^ step) * own_slots + slot]
+                start = pl.multiple_of(kind * columns + offset, 128)
+                into = (4 * at + step, place, place + width)
+                copy = pltpu.make_async_copy(
+                    source.at[:, pl.ds(start, width)],
+                    landed[into[0]].at[:, place : place + width],
+                    sems.at[3 + len(blocks)],
+                )
+                copy.start()
+                blocks.append((copy, kind, *into))
+    small[1].wait()
+    small[2].wait()
+    row = lax.broadcasted_iota(jnp.int32, (rows, band), 0)
+    lane = lax.broadcasted_iota(jnp.int32, (rows, band), 1)
+    weight = jnp.sum(
+        jnp.where(lane == row + wave * rows, gauss_ref[...][None, :], 0.0), axis=1, keepdims=True
+    )
+    row = lax.broadcasted_iota(jnp.int32, (rows, rows), 0)
+    lane = lax.broadcasted_iota(jnp.int32, (rows, rows), 1)
+    points = jnp.sum(
+        jnp.where(lane == row, points_ref[...].astype(jnp.float32)[None, :], 0.0),
+        axis=1,
+        keepdims=True,
+    )
+    if masks:
+        limit_ref = refs[count]
+        for slot in range(own_slots):
+            limit_ref[:, slot * columns : (slot + 1) * columns] = jnp.full(
+                (limit_ref.shape[0], columns), owner_ref[wave * own_slots + slot] * stride, jnp.int32
+            )
+    for copy, kind, at, start, stop in blocks:
+        copy.wait()
+        kept = points >= (2 * kind * stride + 2).astype(jnp.float32)
+        value = jnp.where(kept, landed[at][:, start:stop].astype(jnp.float32) * weight, 0.0)
+        results[at][:, start:stop] = value.astype(jnp.bfloat16)
+
+
+def prepare(fourier, row_points, owner_order, gauss_weight, own_slots, stride, chunks, masks):
+    rows = fourier.shape[0]
+    columns = fourier.shape[1] // owner_order.shape[0]
+    blocks = [(rows, last - first) for first, last in chunks for _ in range(4)]
+    copies = 4 * sum(len(units(first, last, columns)) for first, last in chunks)
+    limits = [jax.ShapeDtypeStruct((8, own_slots * columns), jnp.int32)] * masks
+    outs = pl.pallas_call(
+        functools.partial(prepare_body, stride, own_slots, chunks, masks),
+        in_specs=[pl.BlockSpec(memory_space=pltpu.HBM)] * 4,
+        out_specs=[WHOLE] * (len(blocks) + masks),
+        out_shape=[jax.ShapeDtypeStruct(block, jnp.bfloat16) for block in blocks] + limits,
+        scratch_shapes=[pltpu.VMEM(block, jnp.bfloat16) for block in blocks]
+        + [
+            pltpu.SMEM(owner_order.shape, jnp.int32),
+            pltpu.VMEM(gauss_weight.shape, jnp.float32),
+            pltpu.VMEM(row_points.shape, jnp.int32),
+            pltpu.SemaphoreType.DMA((3 + copies,)),
+        ],
+        compiler_params=PARAMS,
+        cost_estimate=SMALL,
+        name="prepare",
+    )(
+        *[
+            pltpu.with_memory_space_constraint(array, pltpu.HBM)
+            for array in (owner_order, gauss_weight, row_points, fourier)
+        ],
+    )
+    return outs
+
+
+def turn_body(slot, rows, table_hbm, out_ref, table_ref, sem):
+    wave = lax.axis_index("wave")
+    copy = pltpu.make_async_copy(table_hbm.at[slot], table_ref, sem)
+    copy.start()
+    copy.wait()
+    for step in range(4):
+        start = pl.multiple_of((wave ^ step) * rows, 16)
+        out_ref[:, step * rows : (step + 1) * rows] = table_ref[pl.ds(start, rows), :].T
+
+
+def turn(table, slot, rows):
+    _, band, degrees = table.shape
+    return pl.pallas_call(
+        functools.partial(turn_body, slot, rows),
+        in_specs=[pl.BlockSpec(memory_space=pltpu.HBM)],
+        out_specs=WHOLE,
+        out_shape=jax.ShapeDtypeStruct((degrees, band), table.dtype),
+        scratch_shapes=[pltpu.VMEM((band, degrees), table.dtype), pltpu.SemaphoreType.DMA],
+        compiler_params=PARAMS,
+        cost_estimate=SMALL,
+        name="turn",
+    )(pltpu.with_memory_space_constraint(table, pltpu.HBM))
+
+
+def multiply_body(other, parts, *refs):
+    tables, (own, one, two, three, out_ref) = refs[:-5], refs[-5:]
+    share = out_ref.shape[1]
+    core = lax.axis_index("lat") & 1
+    for table_ref, (_, _, width, place) in zip(tables, parts):
+        rows = jnp.concatenate(
+            [piece[:, place : place + width] for piece in (own, one, two, three)], axis=0
+        )
+        for half in range(2):
+            start = pl.multiple_of((2 * half + (1 - core if other else core)) * share, 16)
+            out_ref[half, :, place : place + width] = jnp.dot(
+                table_ref[pl.ds(start, share), :], rows, preferred_element_type=jnp.float32
+            ).astype(out_ref.dtype)
+
+
+def multiply(tables, parts, pieces, other):
+    width = pieces[0].shape[1]
+    share = tables[0].shape[0] // 4
+    return pl.pallas_call(
+        functools.partial(multiply_body, other, parts),
+        in_specs=[WHOLE] * (len(tables) + 4),
+        out_specs=WHOLE,
+        out_shape=jax.ShapeDtypeStruct(
+            (2, share, width), jnp.bfloat16 if other else jnp.float32
+        ),
+        compiler_params=PARAMS,
+        cost_estimate=SMALL if other else LARGE,
+        name="multiply_other" if other else "multiply_own",
+    )(*tables, *pieces)
+
+
+def combine_body(keep_ref, got_ref, send_ref):
+    near = 1 - (lax.axis_index("lat") >> 1)
+    send_ref[...] = (keep_ref[near] + got_ref[near].astype(jnp.float32)).astype(jnp.bfloat16)
+
+
+def combine(keep, got):
+    return pl.pallas_call(
+        combine_body,
+        in_specs=[WHOLE] * 2,
+        out_specs=WHOLE,
+        out_shape=jax.ShapeDtypeStruct(keep.shape[1:], jnp.bfloat16),
+        compiler_params=PARAMS,
+        cost_estimate=SMALL,
+        name="combine",
+    )(keep, got)
+
+
+def finish_body(first, limit_ref, keep_ref, near_ref, far_ref, *refs):
+    out_ref, total_ref, sem = refs[-3:]
+    share, width = total_ref.shape
+    lat = lax.axis_index("lat")
+    far = lat >> 1
+    degree = lat * share + lax.broadcasted_iota(jnp.int32, (share, width), 0)
+    total = keep_ref[far] + near_ref[far].astype(jnp.float32) + far_ref[...].astype(jnp.float32)
+    total_ref[...] = jnp.where(degree >= limit_ref[0:1, first : first + width], total, 0.0)
+    copy = pltpu.make_async_copy(total_ref, out_ref.at[:, first : first + width], sem)
+    copy.start()
+    copy.wait()
+
+
+def finish(limits, keep, near, far, before, first):
+    _, share, width = keep.shape
+    old = [] if before is None else [before]
+    hbm = pl.BlockSpec(memory_space=pltpu.HBM)
+    return pl.pallas_call(
+        functools.partial(finish_body, first),
+        in_specs=[WHOLE] * 4 + [hbm] * len(old),
+        out_specs=hbm,
+        out_shape=pltpu.HBM((share, limits.shape[1]), jnp.float32),
+        input_output_aliases={4: 0} if old else {},
+        scratch_shapes=[pltpu.VMEM((share, width), jnp.float32), pltpu.SemaphoreType.DMA],
+        compiler_params=PARAMS,
+        cost_estimate=SMALL,
+        name="finish",
+    )(limits, keep, near, far, *old)
+
+
+def piped(fourier, row_points, owner_order, gauss_weight, table):
+    slot_total = owner_order.shape[0]
+    own_slots, _, degrees = table.shape
+    stride = degrees // slot_total
+    columns = fourier.shape[1] // slot_total
+    grain = own_slots * columns // 16
+    chunks = [(first * grain, last * grain) for first, last in zip((0,) + CUTS, CUTS + (16,))]
+    count = len(chunks)
+    scalars = (fourier, row_points, owner_order, gauss_weight, own_slots, stride)
+    held = Held(table=table)
+    queue = [(at, step) for at in range(count) for step in STEPS]
+
+    def ready(first, last):
+        masks = int(last == count)
+        outs = prepare(*scalars, chunks[first:last], masks)
+        for at in range(first, last):
+            for step in range(4):
+                name = "piece" if step else "row"
+                held[name, at, step] = outs[4 * (at - first) + step]
+        if masks:
+            held["limits"] = outs[-1]
+
+    def send(place):
+        at, step = queue[place]
+        if place >= WINDOW:
+            held.tie(("piece", at, step), ("row", *queue[place - WINDOW]))
+        held["row", at, step] = exchange(held["piece", at, step], "wave", step)
+
+    def sums(at, other):
+        parts = units(*chunks[at], columns)
+        rows = [held["row", at, step] for step in range(4)]
+        return multiply([held["turned", part[0]] for part in parts], parts, rows, other)
+
+    def multiply_other(at):
+        held["other", at] = sums(at, True)
+
+    def pass_core(at):
+        held["near", at] = exchange(held["other", at], "lat", 1)
+
+    def multiply_own(at):
+        held["keep", at] = sums(at, False)
+
+    def join(at):
+        held["sent", at] = combine(held["keep", at], held["near", at])
+
+    def pass_on(at):
+        held["far", at] = exchange(held["sent", at], "lat", 2)
+
+    def close(at):
+        held["out"] = finish(
+            held["limits"],
+            held["keep", at],
+            held["near", at],
+            held["far", at],
+            held.get("out"),
+            chunks[at][0],
+        )
+
+    ready(0, 1)
+    for place in range(3):
+        send(place)
+    ready(1, count)
+
+    def turn_slots(first, last):
+        for slot in range(first, last):
+            held["turned", slot] = turn(held["table"], slot, fourier.shape[0])
+
+    held.tie("table", ("piece", 1, STEPS[0]))
+    turn_slots(0, EARLY)
+    held.tie(*[("piece", 1, step) for step in STEPS[1:]], "table")
+    for place in range(3, 6):
+        send(place)
+    for at in range(count):
+        if at >= 2:
+            held.tie(("row", at, 0), "out")
+        multiply_other(at)
+        pass_core(at)
+        held.tie(("row", at, 0), ("other", at))
+        multiply_own(at)
+        join(at)
+        if at + 2 < count:
+            held.tie(*[("piece", at + 2, step) for step in STEPS], ("sent", at))
+        pass_on(at)
+        if at == 0:
+            held.tie("table", ("sent", at))
+            turn_slots(EARLY, own_slots)
+        for place in range(3 * at + 6, min(3 * at + 9, len(queue))):
+            send(place)
+        if at >= 1:
+            held.tie(("far", at - 1), ("sent", at))
+            close(at - 1)
+    close(count - 1)
+    return held["out"]
+
+
 def solution(mesh):
     in_specs = (
         P(("grp", "lat", "wave"), None),
@@ -44,6 +363,19 @@
         P("wave", "lat", None),
     )
     out_specs = P(("grp", "lat"), "wave")
+
+    def per_device(fourier, row_points, owner_order, gauss_weight, table):
+        columns = fourier.shape[1] // owner_order.shape[0]
+        four = mesh.shape["wave"] == 4 and mesh.shape["lat"] == 4
+        whole = (
+            table.shape[0] == 4
+            and fourier.shape[0] % 16 == 0
+            and (table.shape[2] // 4) % 16 == 0
+            and columns % 512 == 0
+        )
+        body = piped if four and whole else plain
+        return body(fourier, row_points, owner_order, gauss_weight, table)
+
     return jax.shard_map(
         per_device, mesh=mesh, in_specs=in_specs, out_specs=out_specs, check_vma=False
     )

time: 222 us -> 87.4 us (0.39)
  blocking collectives: 65.6 us -> 0 us
  waiting for transfers between devices: 83 us -> 33.1 us
  local copies, waits for them, and re-layouts: 31.6 us -> 0 us
  starting transfers between devices: 0.01 us -> 27.9 us
  Pallas kernels: 0 us -> 25.7 us
  other arithmetic: 17.5 us -> 0 us
  between operations: 13.5 us -> 0.32 us
  matrix products: 9.93 us -> 0 us
    reduce_scatter x1 -> x0, waiting for transfers between devices: 83 us -> none  [per_device(): lax.psum_scatter(product.reshape(degrees, own_slots * columns), 'lat', sc...]
    all_to_all x1 -> x0, blocking collectives: 65.6 us -> none  [per_device(): lax.all_to_all(ordered, 'wave', split_axis=1, concat_axis=0, tiled=True)]
    ppermute x0 -> x25, waiting for transfers between devices: none -> 33.1 us  [exchange(): return lax.ppermute(value, axis, [(i, i ^ step) for i in range(size)])]
    ppermute x0 -> x25, starting transfers between devices: none -> 27.9 us  [exchange(): return lax.ppermute(value, axis, [(i, i ^ step) for i in range(size)])]
    pallas_call x0 -> x26, Pallas kernels: none -> 25.7 us  [the longest x4 10.8 us: turn(): pl.pallas_call(functools.partial(turn_body, slot, rows), in_specs=[pl.Blo...]
    reshape x1 -> x0, local copies, waits for them, and re-layouts: 11.4 us -> none  [per_device(): product.reshape(degrees, own_slots * columns)]
    dot_general x1 -> x0, matrix products: 9.93 us -> none  [per_device(): jnp.einsum('sjn,jsc->nsc', table, weighted, preferred_element_type=jnp.fl...]
    gather x3 -> x0, local copies, waits for them, and re-layouts: 9.55 us -> none  [per_device(): jnp.take(spread, owner_order, axis=1)]
  transfers between devices with their start and end apart: 1 -> 25, of which waited for: 1 -> 10; matrix products, arithmetic and copies ran while one was open for 0% -> 0% of each run, Pallas kernels for 0% -> 25%
where the time goes in v2:
time: 87.4 us; the launch traced here: 87.1 us
  waiting for transfers between devices  33.1 us (38%)
  starting transfers between devices  27.9 us (32%)
  Pallas kernels  25.7 us (29%)
    ppermute x25, waiting for transfers between devices, exchange(): return lax.ppermute(value, axis, [(i, i ^ step) for i in range(size)])  33.1 us
    ppermute x25, starting transfers between devices, exchange(): return lax.ppermute(value, axis, [(i, i ^ step) for i in range(size)])  27.9 us
    pallas_call x4, Pallas kernels, turn(): pl.pallas_call(functools.partial(turn_body, slot, rows), in_specs=[pl.Blo...  10.8 us
    pallas_call x10, Pallas kernels, multiply(): pl.pallas_call(functools.partial(multiply_body, other, parts), in_specs=[...  5.65 us
    pallas_call x5, Pallas kernels, finish(): pl.pallas_call(functools.partial(finish_body, first), in_specs=[WHOLE] *...  4.59 us
    pallas_call x2, Pallas kernels, prepare(): pl.pallas_call(functools.partial(prepare_body, stride, own_slots, chunks,...  4.41 us
  transfers between devices with their start and end apart: 25, of which 10 were waited for; matrix products, arithmetic and copies ran while one was open for 0% of the time, Pallas kernels for 25%

profile of v2, /device:TPU:0, one launch (start us, length us, event | category | flops | bytes accessed | tf_op | source)
XLA Modules:
  0.0 87.1 jit_solution(633463728244138270)
XLA Ops:
  0.0 1.9 %prepare.3 = (bf16[160,512]{1,0:T(8,128)(2,1)S(1)}, bf16[160,512]{1,0:T(8,128)(2,1)S(1)}, bf16[160,512]{1,0:T(8,128)(2,1)S(1)}, bf16[160,512]{1,0:T(8,128)(2,1)S(1)}) custom-call(s32[16]{0:T(128)} %owner_hbm.3, f32[640]{0:T(1024)} %gauss_hbm.3, s32[160]{0:T(256)} %points_hbm.3, bf16[160,8192]{1,0:T(8,128)(2,1)} %source.3), custom_call_target="tpu_custom_call" | custom-call | flops 1 | bytes 1 | tf_op jit(solution)/shard_map/prepare/pallas_call | solution.py:136
  1.9 3.1 %collective-permute-start = (bf16[160,512]{1,0:T(8,128)(2,1)S(1)}, bf16[160,512]{1,0:T(8,128)(2,1)S(1)}, u32[]{:S(2)}, u32[]{:S(2)}) collective-permute-start(bf16[160,512]{1,0:T(8,128)(2,1)S(1)} %get-tuple-element.78), channel_id=1, source_target_pairs={{0,4},{4,0},{8,12},{12,8},{1,5},{5,1},{9,13},{13,9},{2,6},{6,2},{1... | collective-permute-start | bytes 491528 | tf_op jit(solution)/shard_map/wave_1/ppermute | solution.py:55
  5.0 2.6 %collective-permute-start.1 = (bf16[160,512]{1,0:T(8,128)(2,1)S(1)}, bf16[160,512]{1,0:T(8,128)(2,1)S(1)}, u32[]{:S(2)}, u32[]{:S(2)}) collective-permute-start(bf16[160,512]{1,0:T(8,128)(2,1)S(1)} %get-tuple-element.79), channel_id=1, source_target_pairs={{0,8},{4,12},{8,0},{12,4},{1,9},{5,13},{9,1},{13,5},{2,10},{6,14},... | collective-permute-start | bytes 491528 | tf_op jit(solution)/shard_map/wave_2/ppermute | solution.py:55
  7.6 2.5 %prepare.2 = (bf16[160,512]{1,0:T(8,128)(2,1)S(1)}, bf16[160,512]{1,0:T(8,128)(2,1)S(1)}, bf16[160,512]{1,0:T(8,128)(2,1)S(1)}, bf16[160,512]{1,0:T(8,128)(2,1)S...) custom-call(s32[16]{0:T(128)} %owner_hbm.3, ...), custom_call_target="tpu_custom_call" | custom-call | flops 1 | bytes 1 | tf_op jit(solution)/shard_map/prepare/pallas_call | solution.py:136
  11.1 3.0 %collective-permute-start.7 = (bf16[160,512]{1,0:T(8,128)(2,1)S(1)}, bf16[160,512]{1,0:T(8,128)(2,1)S(1)}, u32[]{:S(2)}, u32[]{:S(2)}) collective-permute-start(bf16[160,512]{1,0:T(8,128)(2,1)S(1)} %get-tuple-element.92), channel_id=1, source_target_pairs={{0,12},{4,8},{8,4},{12,0},{1,13},{5,9},{9,5},{13,1},{2,14},{6,10},... | collective-permute-start | bytes 491528 | tf_op jit(solution)/shard_map/wave_3/ppermute | solution.py:55
  14.6 2.7 %turn.7.refs_0_ = bf16[1280,640]{1,0:T(8,128)(2,1)S(1)} custom-call(bf16[4,640,1280]{2,1,0:T(8,128)(2,1)} %table_hbm.3), custom_call_target="tpu_custom_call" | custom-call | flops 1 | bytes 1 | tf_op jit(solution)/shard_map/turn/pallas_call | solution.py:172
  17.3 2.7 %turn.4.refs_0_ = bf16[1280,640]{1,0:T(8,128)(2,1)S(1)} custom-call(bf16[4,640,1280]{2,1,0:T(8,128)(2,1)} %table_hbm.3), custom_call_target="tpu_custom_call" | custom-call | flops 1 | bytes 1 | tf_op jit(solution)/shard_map/turn/pallas_call | solution.py:172
  20.9 5.9 %collective-permute-done.7.refs_4_ = bf16[160,512]{1,0:T(8,128)(2,1)S(1)} collective-permute-done((bf16[160,512]{1,0:T(8,128)(2,1)S(1)}, bf16[160,512]{1,0:T(8,128)(2,1)S(1)}, u32[]{:S(2)}, u32[]{:S(2)}) %collective-permute-start.7) | collective-permute-done | bytes 163872 | tf_op jit(solution)/shard_map/wave_3/ppermute | solution.py:55
  26.8 9.5 %collective-permute-done.6.refs_3_ = bf16[160,512]{1,0:T(8,128)(2,1)S(1)} collective-permute-done((bf16[160,512]{1,0:T(8,128)(2,1)S(1)}, bf16[160,512]{1,0:T(8,128)(2,1)S(1)}, u32[]{:S(2)}, u32[]{:S(2)}) %collective-permute-start.6) | collective-permute-done | bytes 163872 | tf_op jit(solution)/shard_map/wave_2/ppermute | solution.py:55
  37.8 1.6 %collective-permute-start.4 = (bf16[320,512]{1,0:T(8,128)(2,1)S(1)}, bf16[320,512]{1,0:T(8,128)(2,1)S(1)}, u32[]{:S(2)}, u32[]{:S(2)}) collective-permute-start(bf16[320,512]{1,0:T(8,128)(2,1)S(1)} %combine.5), channel_id=1, source_target_pairs={{0,2},{1,3},{2,0},{3,1},{4,6},{5,7},{6,4},{7,5},{8,10},{9,11},{10,... | collective-permute-start | bytes 983048 | tf_op jit(solution)/shard_map/lat_2/ppermute | solution.py:55
  39.3 2.5 %collective-permute-start.11 = (bf16[160,512]{1,0:T(8,128)(2,1)S(1)}, bf16[160,512]{1,0:T(8,128)(2,1)S(1)}, u32[]{:S(2)}, u32[]{:S(2)}) collective-permute-start(bf16[160,512]{1,0:T(8,128)(2,1)S(1)} %get-tuple-element.102), channel_id=1, source_target_pairs={{0,12},{4,8},{8,4},{12,0},{1,13},{5,9},{9,5},{13,1},{2,14},{6,10},... | collective-permute-start | bytes 491528 | tf_op jit(solution)/shard_map/wave_3/ppermute | solution.py:55
  43.5 2.7 %turn.6.refs_0_ = bf16[1280,640]{1,0:T(8,128)(2,1)S(1)} custom-call(bf16[4,640,1280]{2,1,0:T(8,128)(2,1)} %table_hbm.3), custom_call_target="tpu_custom_call" | custom-call | flops 1 | bytes 1 | tf_op jit(solution)/shard_map/turn/pallas_call | solution.py:172
  46.2 2.7 %turn.5.refs_0_ = bf16[1280,640]{1,0:T(8,128)(2,1)S(1)} custom-call(bf16[4,640,1280]{2,1,0:T(8,128)(2,1)} %table_hbm.3), custom_call_target="tpu_custom_call" | custom-call | flops 1 | bytes 1 | tf_op jit(solution)/shard_map/turn/pallas_call | solution.py:172
  49.6 1.0 %collective-permute-start.15 = (bf16[160,256]{1,0:T(8,128)(2,1)S(1)}, bf16[160,256]{1,0:T(8,128)(2,1)S(1)}, u32[]{:S(2)}, u32[]{:S(2)}) collective-permute-start(bf16[160,256]{1,0:T(8,128)(2,1)S(1)} %get-tuple-element.113), channel_id=1, source_target_pairs={{0,4},{4,0},{8,12},{12,8},{1,5},{5,1},{9,13},{13,9},{2,6},{6,2},{1... | collective-permute-start | bytes 245768 | tf_op jit(solution)/shard_map/wave_1/ppermute | solution.py:55
  51.6 1.9 %collective-permute-done.10.refs_3_ = bf16[160,512]{1,0:T(8,128)(2,1)S(1)} collective-permute-done((bf16[160,512]{1,0:T(8,128)(2,1)S(1)}, bf16[160,512]{1,0:T(8,128)(2,1)S(1)}, u32[]{:S(2)}, u32[]{:S(2)}) %collective-permute-start.10) | collective-permute-done | bytes 163872 | tf_op jit(solution)/shard_map/wave_2/ppermute | solution.py:55
  53.5 1.4 %collective-permute-start.17 = (bf16[160,256]{1,0:T(8,128)(2,1)S(1)}, bf16[160,256]{1,0:T(8,128)(2,1)S(1)}, u32[]{:S(2)}, u32[]{:S(2)}) collective-permute-start(bf16[160,256]{1,0:T(8,128)(2,1)S(1)} %get-tuple-element.117), channel_id=1, source_target_pairs={{0,12},{4,8},{8,4},{12,0},{1,13},{5,9},{9,5},{13,1},{2,14},{6,10},... | collective-permute-start | bytes 245768 | tf_op jit(solution)/shard_map/wave_3/ppermute | solution.py:55
  54.9 2.6 %collective-permute-start.16 = (bf16[160,256]{1,0:T(8,128)(2,1)S(1)}, bf16[160,256]{1,0:T(8,128)(2,1)S(1)}, u32[]{:S(2)}, u32[]{:S(2)}) collective-permute-start(bf16[160,256]{1,0:T(8,128)(2,1)S(1)} %get-tuple-element.115), channel_id=1, source_target_pairs={{0,8},{4,12},{8,0},{12,4},{1,9},{5,13},{9,1},{13,5},{2,10},{6,14},... | collective-permute-start | bytes 245768 | tf_op jit(solution)/shard_map/wave_2/ppermute | solution.py:55
  58.9 1.4 %collective-permute-done.12.got_ref.near_ref = bf16[2,320,512]{2,1,0:T(8,128)(2,1)S(1)} collective-permute-done((bf16[2,320,512]{2,1,0:T(8,128)(2,1)S(1)}, bf16[2,320,512]{2,1,0:T(8,128)(2,1)S(1)}, u32[]{:S(2)}, u32[]{:S(2)}) %collective-permute-start.12) | collective-permute-done | bytes 655392 | tf_op jit(solution)/shard_map/lat_1/ppermute | solution.py:55
  61.4 2.6 %collective-permute-done.16.refs_3_ = bf16[160,256]{1,0:T(8,128)(2,1)S(1)} collective-permute-done((bf16[160,256]{1,0:T(8,128)(2,1)S(1)}, bf16[160,256]{1,0:T(8,128)(2,1)S(1)}, u32[]{:S(2)}, u32[]{:S(2)}) %collective-permute-start.16) | collective-permute-done | bytes 81952 | tf_op jit(solution)/shard_map/wave_2/ppermute | solution.py:55
  65.1 1.4 %collective-permute-start.21 = (bf16[160,256]{1,0:T(8,128)(2,1)S(1)}, bf16[160,256]{1,0:T(8,128)(2,1)S(1)}, u32[]{:S(2)}, u32[]{:S(2)}) collective-permute-start(bf16[160,256]{1,0:T(8,128)(2,1)S(1)} %get-tuple-element.127), channel_id=1, source_target_pairs={{0,12},{4,8},{8,4},{12,0},{1,13},{5,9},{9,5},{13,1},{2,14},{6,10},... | collective-permute-start | bytes 245768 | tf_op jit(solution)/shard_map/wave_3/ppermute | solution.py:55
  66.4 3.0 %collective-permute-start.19 = (bf16[160,256]{1,0:T(8,128)(2,1)S(1)}, bf16[160,256]{1,0:T(8,128)(2,1)S(1)}, u32[]{:S(2)}, u32[]{:S(2)}) collective-permute-start(bf16[160,256]{1,0:T(8,128)(2,1)S(1)} %get-tuple-element.123), channel_id=1, source_target_pairs={{0,4},{4,0},{8,12},{12,8},{1,5},{5,1},{9,13},{13,9},{2,6},{6,2},{1... | collective-permute-start | bytes 245768 | tf_op jit(solution)/shard_map/wave_1/ppermute | solution.py:55
  69.9 4.7 %collective-permute-done.13.far_ref = bf16[320,512]{1,0:T(8,128)(2,1)S(1)} collective-permute-done((bf16[320,512]{1,0:T(8,128)(2,1)S(1)}, bf16[320,512]{1,0:T(8,128)(2,1)S(1)}, u32[]{:S(2)}, u32[]{:S(2)}) %collective-permute-start.13) | collective-permute-done | bytes 327712 | tf_op jit(solution)/shard_map/lat_2/ppermute | solution.py:55
  78.8 4.4 %collective-permute-done.24.far_ref = bf16[320,256]{1,0:T(8,128)(2,1)S(1)} collective-permute-done((bf16[320,256]{1,0:T(8,128)(2,1)S(1)}, bf16[320,256]{1,0:T(8,128)(2,1)S(1)}, u32[]{:S(2)}, u32[]{:S(2)}) %collective-permute-start.24) | collective-permute-done | bytes 163872 | tf_op jit(solution)/shard_map/lat_2/ppermute | solution.py:55
  84.0 2.2 %collective-permute-done.23.far_ref = bf16[320,256]{1,0:T(8,128)(2,1)S(1)} collective-permute-done((bf16[320,256]{1,0:T(8,128)(2,1)S(1)}, bf16[320,256]{1,0:T(8,128)(2,1)S(1)}, u32[]{:S(2)}, u32[]{:S(2)}) %collective-permute-start.23) | collective-permute-done | bytes 163872 | tf_op jit(solution)/shard_map/lat_2/ppermute | solution.py:55
  (52 shorter events, 16.9 us)
Async XLA Ops:
  1.9 12.1 %collective-permute-start = (bf16[160,512]{1,0:T(8,128)(2,1)S(1)}, bf16[160,512]{1,0:T(8,128)(2,1)S(1)}, u32[]{:S(2)}, u32[]{:S(2)}) collective-permute-start(bf16[160,512]{1,0:T(8,128)(2,1)S(1)} %get-tuple-element.78), channel_id=1, source_target_pairs={{0,4},{4,0},{8,12},{12,8},{1,5},{5,1},{9,13},{13,9},{2,6},{6,2},{1... | collective-permute-start | bytes 491528 | tf_op jit(solution)/shard_map/wave_1/ppermute | solution.py:55
  5.0 15.1 %collective-permute-start.1 = (bf16[160,512]{1,0:T(8,128)(2,1)S(1)}, bf16[160,512]{1,0:T(8,128)(2,1)S(1)}, u32[]{:S(2)}, u32[]{:S(2)}) collective-permute-start(bf16[160,512]{1,0:T(8,128)(2,1)S(1)} %get-tuple-element.79), channel_id=1, source_target_pairs={{0,8},{4,12},{8,0},{12,4},{1,9},{5,13},{9,1},{13,5},{2,10},{6,14},... | collective-permute-start | bytes 491528 | tf_op jit(solution)/shard_map/wave_2/ppermute | solution.py:55
  7.6 12.5 %collective-permute-start.2 = (bf16[160,512]{1,0:T(8,128)(2,1)S(1)}, bf16[160,512]{1,0:T(8,128)(2,1)S(1)}, u32[]{:S(2)}, u32[]{:S(2)}) collective-permute-start(bf16[160,512]{1,0:T(8,128)(2,1)S(1)} %get-tuple-element.80), channel_id=1, source_target_pairs={{0,12},{4,8},{8,4},{12,0},{1,13},{5,9},{9,5},{13,1},{2,14},{6,10},... | collective-permute-start | bytes 491528 | tf_op jit(solution)/shard_map/wave_3/ppermute | solution.py:55
  10.1 10.8 %collective-permute-start.5 = (bf16[160,512]{1,0:T(8,128)(2,1)S(1)}, bf16[160,512]{1,0:T(8,128)(2,1)S(1)}, u32[]{:S(2)}, u32[]{:S(2)}) collective-permute-start(bf16[160,512]{1,0:T(8,128)(2,1)S(1)} %get-tuple-element.90), channel_id=1, source_target_pairs={{0,4},{4,0},{8,12},{12,8},{1,5},{5,1},{9,13},{13,9},{2,6},{6,2},{1... | collective-permute-start | bytes 491528 | tf_op jit(solution)/shard_map/wave_1/ppermute | solution.py:55
  11.1 15.7 %collective-permute-start.7 = (bf16[160,512]{1,0:T(8,128)(2,1)S(1)}, bf16[160,512]{1,0:T(8,128)(2,1)S(1)}, u32[]{:S(2)}, u32[]{:S(2)}) collective-permute-start(bf16[160,512]{1,0:T(8,128)(2,1)S(1)} %get-tuple-element.92), channel_id=1, source_target_pairs={{0,12},{4,8},{8,4},{12,0},{1,13},{5,9},{9,5},{13,1},{2,14},{6,10},... | collective-permute-start | bytes 491528 | tf_op jit(solution)/shard_map/wave_3/ppermute | solution.py:55
  14.1 22.2 %collective-permute-start.6 = (bf16[160,512]{1,0:T(8,128)(2,1)S(1)}, bf16[160,512]{1,0:T(8,128)(2,1)S(1)}, u32[]{:S(2)}, u32[]{:S(2)}) collective-permute-start(bf16[160,512]{1,0:T(8,128)(2,1)S(1)} %get-tuple-element.91), channel_id=1, source_target_pairs={{0,8},{4,12},{8,0},{12,4},{1,9},{5,13},{9,1},{13,5},{2,10},{6,14},... | collective-permute-start | bytes 491528 | tf_op jit(solution)/shard_map/wave_2/ppermute | solution.py:55
  20.8 16.9 %collective-permute-start.3 = (bf16[2,320,512]{2,1,0:T(8,128)(2,1)S(1)}, bf16[2,320,512]{2,1,0:T(8,128)(2,1)S(1)}, u32[]{:S(2)}, u32[]{:S(2)}) collective-permute-start(bf16[2,320,512]{2,1,0:T(8,128)(2,1)S(1)} %multiply_other.5), channel_id=1, source_target_pairs={{0,1},{1,0},{2,3},{3,2},{4,5},{5,4},{6,7},{7,6},{8,9},{9,8},{10,11... | collective-permute-start | bytes 1966088 | tf_op jit(solution)/shard_map/lat_1/ppermute | solution.py:55
  36.9 12.0 %collective-permute-start.8 = (bf16[2,320,512]{2,1,0:T(8,128)(2,1)S(1)}, bf16[2,320,512]{2,1,0:T(8,128)(2,1)S(1)}, u32[]{:S(2)}, u32[]{:S(2)}) collective-permute-start(bf16[2,320,512]{2,1,0:T(8,128)(2,1)S(1)} %multiply_other.6), channel_id=1, source_target_pairs={{0,1},{1,0},{2,3},{3,2},{4,5},{5,4},{6,7},{7,6},{8,9},{9,8},{10,11... | collective-permute-start | bytes 1966088 | tf_op jit(solution)/shard_map/lat_1/ppermute | solution.py:55
  37.8 11.8 %collective-permute-start.4 = (bf16[320,512]{1,0:T(8,128)(2,1)S(1)}, bf16[320,512]{1,0:T(8,128)(2,1)S(1)}, u32[]{:S(2)}, u32[]{:S(2)}) collective-permute-start(bf16[320,512]{1,0:T(8,128)(2,1)S(1)} %combine.5), channel_id=1, source_target_pairs={{0,2},{1,3},{2,0},{3,1},{4,6},{5,7},{6,4},{7,5},{8,10},{9,11},{10,... | collective-permute-start | bytes 983048 | tf_op jit(solution)/shard_map/lat_2/ppermute | solution.py:55
  39.3 14.2 %collective-permute-start.10 = (bf16[160,512]{1,0:T(8,128)(2,1)S(1)}, bf16[160,512]{1,0:T(8,128)(2,1)S(1)}, u32[]{:S(2)}, u32[]{:S(2)}) collective-permute-start(bf16[160,512]{1,0:T(8,128)(2,1)S(1)} %get-tuple-element.100), channel_id=1, source_target_pairs={{0,8},{4,12},{8,0},{12,4},{1,9},{5,13},{9,1},{13,5},{2,10},{6,14},... | collective-permute-start | bytes 491528 | tf_op jit(solution)/shard_map/wave_2/ppermute | solution.py:55
  39.3 15.5 %collective-permute-start.11 = (bf16[160,512]{1,0:T(8,128)(2,1)S(1)}, bf16[160,512]{1,0:T(8,128)(2,1)S(1)}, u32[]{:S(2)}, u32[]{:S(2)}) collective-permute-start(bf16[160,512]{1,0:T(8,128)(2,1)S(1)} %get-tuple-element.102), channel_id=1, source_target_pairs={{0,12},{4,8},{8,4},{12,0},{1,13},{5,9},{9,5},{13,1},{2,14},{6,10},... | collective-permute-start | bytes 491528 | tf_op jit(solution)/shard_map/wave_3/ppermute | solution.py:55
  41.8 15.7 %collective-permute-start.9 = (bf16[160,512]{1,0:T(8,128)(2,1)S(1)}, bf16[160,512]{1,0:T(8,128)(2,1)S(1)}, u32[]{:S(2)}, u32[]{:S(2)}) collective-permute-start(bf16[160,512]{1,0:T(8,128)(2,1)S(1)} %get-tuple-element.98), channel_id=1, source_target_pairs={{0,4},{4,0},{8,12},{12,8},{1,5},{5,1},{9,13},{13,9},{2,6},{6,2},{1... | collective-permute-start | bytes 491528 | tf_op jit(solution)/shard_map/wave_1/ppermute | solution.py:55
  49.0 11.4 %collective-permute-start.14 = (bf16[320,512]{1,0:T(8,128)(2,1)S(1)}, bf16[320,512]{1,0:T(8,128)(2,1)S(1)}, u32[]{:S(2)}, u32[]{:S(2)}) collective-permute-start(bf16[320,512]{1,0:T(8,128)(2,1)S(1)} %combine.6), channel_id=1, source_target_pairs={{0,2},{1,3},{2,0},{3,1},{4,6},{5,7},{6,4},{7,5},{8,10},{9,11},{10,... | collective-permute-start | bytes 983048 | tf_op jit(solution)/shard_map/lat_2/ppermute | solution.py:55
  49.6 11.8 %collective-permute-start.15 = (bf16[160,256]{1,0:T(8,128)(2,1)S(1)}, bf16[160,256]{1,0:T(8,128)(2,1)S(1)}, u32[]{:S(2)}, u32[]{:S(2)}) collective-permute-start(bf16[160,256]{1,0:T(8,128)(2,1)S(1)} %get-tuple-element.113), channel_id=1, source_target_pairs={{0,4},{4,0},{8,12},{12,8},{1,5},{5,1},{9,13},{13,9},{2,6},{6,2},{1... | collective-permute-start | bytes 245768 | tf_op jit(solution)/shard_map/wave_1/ppermute | solution.py:55
  53.5 7.9 %collective-permute-start.17 = (bf16[160,256]{1,0:T(8,128)(2,1)S(1)}, bf16[160,256]{1,0:T(8,128)(2,1)S(1)}, u32[]{:S(2)}, u32[]{:S(2)}) collective-permute-start(bf16[160,256]{1,0:T(8,128)(2,1)S(1)} %get-tuple-element.117), channel_id=1, source_target_pairs={{0,12},{4,8},{8,4},{12,0},{1,13},{5,9},{9,5},{13,1},{2,14},{6,10},... | collective-permute-start | bytes 245768 | tf_op jit(solution)/shard_map/wave_3/ppermute | solution.py:55
  54.9 9.1 %collective-permute-start.16 = (bf16[160,256]{1,0:T(8,128)(2,1)S(1)}, bf16[160,256]{1,0:T(8,128)(2,1)S(1)}, u32[]{:S(2)}, u32[]{:S(2)}) collective-permute-start(bf16[160,256]{1,0:T(8,128)(2,1)S(1)} %get-tuple-element.115), channel_id=1, source_target_pairs={{0,8},{4,12},{8,0},{12,4},{1,9},{5,13},{9,1},{13,5},{2,10},{6,14},... | collective-permute-start | bytes 245768 | tf_op jit(solution)/shard_map/wave_2/ppermute | solution.py:55
  58.1 2.2 %collective-permute-start.12 = (bf16[2,320,512]{2,1,0:T(8,128)(2,1)S(1)}, bf16[2,320,512]{2,1,0:T(8,128)(2,1)S(1)}, u32[]{:S(2)}, u32[]{:S(2)}) collective-permute-start(bf16[2,320,512]{2,1,0:T(8,128)(2,1)S(1)} %multiply_other.7), channel_id=1, source_target_pairs={{0,1},{1,0},{2,3},{3,2},{4,5},{5,4},{6,7},{7,6},{8,9},{9,8},{10,11... | collective-permute-start | bytes 1966088 | tf_op jit(solution)/shard_map/lat_1/ppermute | solution.py:55
  64.4 5.5 %collective-permute-start.18 = (bf16[2,320,256]{2,1,0:T(8,128)(2,1)S(1)}, bf16[2,320,256]{2,1,0:T(8,128)(2,1)S(1)}, u32[]{:S(2)}, u32[]{:S(2)}) collective-permute-start(bf16[2,320,256]{2,1,0:T(8,128)(2,1)S(1)} %multiply_other.8), channel_id=1, source_target_pairs={{0,1},{1,0},{2,3},{3,2},{4,5},{5,4},{6,7},{7,6},{8,9},{9,8},{10,11... | collective-permute-start | bytes 983048 | tf_op jit(solution)/shard_map/lat_1/ppermute | solution.py:55
  64.5 10.1 %collective-permute-start.13 = (bf16[320,512]{1,0:T(8,128)(2,1)S(1)}, bf16[320,512]{1,0:T(8,128)(2,1)S(1)}, u32[]{:S(2)}, u32[]{:S(2)}) collective-permute-start(bf16[320,512]{1,0:T(8,128)(2,1)S(1)} %combine.7), channel_id=1, source_target_pairs={{0,2},{1,3},{2,0},{3,1},{4,6},{5,7},{6,4},{7,5},{8,10},{9,11},{10,... | collective-permute-start | bytes 983048 | tf_op jit(solution)/shard_map/lat_2/ppermute | solution.py:55
  65.1 10.5 %collective-permute-start.21 = (bf16[160,256]{1,0:T(8,128)(2,1)S(1)}, bf16[160,256]{1,0:T(8,128)(2,1)S(1)}, u32[]{:S(2)}, u32[]{:S(2)}) collective-permute-start(bf16[160,256]{1,0:T(8,128)(2,1)S(1)} %get-tuple-element.127), channel_id=1, source_target_pairs={{0,12},{4,8},{8,4},{12,0},{1,13},{5,9},{9,5},{13,1},{2,14},{6,10},... | collective-permute-start | bytes 245768 | tf_op jit(solution)/shard_map/wave_3/ppermute | solution.py:55
  66.4 9.2 %collective-permute-start.20 = (bf16[160,256]{1,0:T(8,128)(2,1)S(1)}, bf16[160,256]{1,0:T(8,128)(2,1)S(1)}, u32[]{:S(2)}, u32[]{:S(2)}) collective-permute-start(bf16[160,256]{1,0:T(8,128)(2,1)S(1)} %get-tuple-element.125), channel_id=1, source_target_pairs={{0,8},{4,12},{8,0},{12,4},{1,9},{5,13},{9,1},{13,5},{2,10},{6,14},... | collective-permute-start | bytes 245768 | tf_op jit(solution)/shard_map/wave_2/ppermute | solution.py:55
  66.4 9.2 %collective-permute-start.19 = (bf16[160,256]{1,0:T(8,128)(2,1)S(1)}, bf16[160,256]{1,0:T(8,128)(2,1)S(1)}, u32[]{:S(2)}, u32[]{:S(2)}) collective-permute-start(bf16[160,256]{1,0:T(8,128)(2,1)S(1)} %get-tuple-element.123), channel_id=1, source_target_pairs={{0,4},{4,0},{8,12},{12,8},{1,5},{5,1},{9,13},{13,9},{2,6},{6,2},{1... | collective-permute-start | bytes 245768 | tf_op jit(solution)/shard_map/wave_1/ppermute | solution.py:55
  76.1 7.1 %collective-permute-start.24 = (bf16[320,256]{1,0:T(8,128)(2,1)S(1)}, bf16[320,256]{1,0:T(8,128)(2,1)S(1)}, u32[]{:S(2)}, u32[]{:S(2)}) collective-permute-start(bf16[320,256]{1,0:T(8,128)(2,1)S(1)} %combine.8), channel_id=1, source_target_pairs={{0,2},{1,3},{2,0},{3,1},{4,6},{5,7},{6,4},{7,5},{8,10},{9,11},{10,... | collective-permute-start | bytes 491528 | tf_op jit(solution)/shard_map/lat_2/ppermute | solution.py:55
  77.8 8.5 %collective-permute-start.23 = (bf16[320,256]{1,0:T(8,128)(2,1)S(1)}, bf16[320,256]{1,0:T(8,128)(2,1)S(1)}, u32[]{:S(2)}, u32[]{:S(2)}) collective-permute-start(bf16[320,256]{1,0:T(8,128)(2,1)S(1)} %combine.9), channel_id=1, source_target_pairs={{0,2},{1,3},{2,0},{3,1},{4,6},{5,7},{6,4},{7,5},{8,10},{9,11},{10,... | collective-permute-start | bytes 491528 | tf_op jit(solution)/shard_map/lat_2/ppermute | solution.py:55
  (1 other events, 1.7 us)

commit v3 on v2

--- a/solution.py
+++ b/solution.py
@@ -10,12 +10,17 @@
 WHOLE = pl.BlockSpec(memory_space=pltpu.VMEM)
 SCALARS = pl.BlockSpec(memory_space=pltpu.SMEM)
 PARAMS = pltpu.CompilerParams(vmem_limit_bytes=48 * 2**20)
-LARGE = pl.CostEstimate(flops=20_000_000_000, transcendentals=0, bytes_accessed=1)
+LARGE = pl.CostEstimate(flops=1, transcendentals=0, bytes_accessed=1)
+HUGE = pl.CostEstimate(flops=20000000000, transcendentals=0, bytes_accessed=1)
 SMALL = pl.CostEstimate(flops=1, transcendentals=0, bytes_accessed=1)
 WINDOW = 6
 EARLY = 2
+PINS = ('sent', 'none', 'none', 'none')
+OUTS = 1
+SEQ = (1, 1, 1, 1, 1)
+CLOSE = 1
 STEPS = (2, 3, 1)
-CUTS = (4, 8, 12, 14)
+CUTS = (4, 8, 12)
 
 
 def plain(fourier, row_points, owner_order, gauss_weight, table):
@@ -207,7 +212,7 @@
             (2, share, width), jnp.bfloat16 if other else jnp.float32
         ),
         compiler_params=PARAMS,
-        cost_estimate=SMALL if other else LARGE,
+        cost_estimate=LARGE if other else HUGE,
         name="multiply_other" if other else "multiply_own",
     )(*tables, *pieces)
 
@@ -331,26 +336,34 @@
     held.tie(*[("piece", 1, step) for step in STEPS[1:]], "table")
     for place in range(3, 6):
         send(place)
+    def hold(at, name):
+        if at + 2 < count and PINS[at] == name:
+            held.tie(*[("piece", at + 2, step) for step in STEPS], (name, at))
+
     for at in range(count):
-        if at >= 2:
+        if at >= 2 and OUTS:
             held.tie(("row", at, 0), "out")
+        if at >= 1 and SEQ[at - 1]:
+            held.tie(("row", at, 0), ("sent", at - 1))
         multiply_other(at)
+        hold(at, "other")
         pass_core(at)
         held.tie(("row", at, 0), ("other", at))
         multiply_own(at)
+        hold(at, "keep")
         join(at)
-        if at + 2 < count:
-            held.tie(*[("piece", at + 2, step) for step in STEPS], ("sent", at))
+        hold(at, "sent")
         pass_on(at)
         if at == 0:
             held.tie("table", ("sent", at))
             turn_slots(EARLY, own_slots)
         for place in range(3 * at + 6, min(3 * at + 9, len(queue))):
             send(place)
-        if at >= 1:
-            held.tie(("far", at - 1), ("sent", at))
-            close(at - 1)
-    close(count - 1)
+        if at >= CLOSE:
+            held.tie(("far", at - CLOSE), ("sent", at))
+            close(at - CLOSE)
+    for at in range(count - CLOSE, count):
+        close(at)
     return held["out"]
 
 

time: 87.4 us -> 82.2 us (0.941)
  starting transfers between devices: 27.9 us -> 22.8 us
  Pallas kernels: 25.7 us -> 24.7 us
  waiting for transfers between devices: 33.1 us -> 34 us
    ppermute x25 -> x20, starting transfers between devices: 27.9 us -> 22.8 us  [exchange(): return lax.ppermute(value, axis, [(i, i ^ step) for i in range(size)])]
    ppermute x25 -> x20, waiting for transfers between devices: 33.1 us -> 34 us  [exchange(): return lax.ppermute(value, axis, [(i, i ^ step) for i in range(size)])]
    pallas_call x5 -> x4, Pallas kernels: 4.59 us -> 3.95 us  [finish(): pl.pallas_call(functools.partial(finish_body, first), in_specs=[WHOLE] *...]
    pallas_call x10 -> x8, Pallas kernels: 5.65 us -> 5.34 us  [multiply(): pl.pallas_call(functools.partial(multiply_body, other, parts), in_specs=[...]
  transfers between devices with their start and end apart: 25 -> 20, of which waited for: 10 -> 9; matrix products, arithmetic and copies ran while one was open for 0% -> 0% of each run, Pallas kernels for 25% -> 27%
where the time goes in v3:
time: 82.2 us; the launch traced here: 81.8 us
  waiting for transfers between devices  34 us (41%)
  Pallas kernels  24.7 us (30%)
  starting transfers between devices  22.8 us (28%)
    ppermute x20, waiting for transfers between devices, exchange(): return lax.ppermute(value, axis, [(i, i ^ step) for i in range(size)])  34 us
    ppermute x20, starting transfers between devices, exchange(): return lax.ppermute(value, axis, [(i, i ^ step) for i in range(size)])  22.8 us
    pallas_call x4, Pallas kernels, turn(): pl.pallas_call(functools.partial(turn_body, slot, rows), in_specs=[pl.Blo...  10.8 us
    pallas_call x8, Pallas kernels, multiply(): pl.pallas_call(functools.partial(multiply_body, other, parts), in_specs=[...  5.34 us
    pallas_call x2, Pallas kernels, prepare(): pl.pallas_call(functools.partial(prepare_body, stride, own_slots, chunks,...  4.37 us
    pallas_call x4, Pallas kernels, finish(): pl.pallas_call(functools.partial(finish_body, first), in_specs=[WHOLE] *...  3.95 us
  transfers between devices with their start and end apart: 20, of which 9 were waited for; matrix products, arithmetic and copies ran while one was open for 0% of the time, Pallas kernels for 27%

profile of v3, /device:TPU:0, one launch (start us, length us, event | category | flops | bytes accessed | tf_op | source)
XLA Modules:
  0.0 81.8 jit_solution(8423277009557595377)
XLA Ops:
  0.0 1.9 %prepare.3 = (bf16[160,512]{1,0:T(8,128)(2,1)S(1)}, bf16[160,512]{1,0:T(8,128)(2,1)S(1)}, bf16[160,512]{1,0:T(8,128)(2,1)S(1)}, bf16[160,512]{1,0:T(8,128)(2,1)S(1)}) custom-call(s32[16]{0:T(128)} %owner_hbm.3, f32[640]{0:T(1024)} %gauss_hbm.3, s32[160]{0:T(256)} %points_hbm.3, bf16[160,8192]{1,0:T(8,128)(2,1)} %source.3), custom_call_target="tpu_custom_call" | custom-call | flops 1 | bytes 1 | tf_op jit(solution)/shard_map/prepare/pallas_call | solution.py:141
  1.9 3.1 %collective-permute-start = (bf16[160,512]{1,0:T(8,128)(2,1)S(1)}, bf16[160,512]{1,0:T(8,128)(2,1)S(1)}, u32[]{:S(2)}, u32[]{:S(2)}) collective-permute-start(bf16[160,512]{1,0:T(8,128)(2,1)S(1)} %get-tuple-element.59), channel_id=1, source_target_pairs={{0,4},{4,0},{8,12},{12,8},{1,5},{5,1},{9,13},{13,9},{2,6},{6,2},{1... | collective-permute-start | bytes 491528 | tf_op jit(solution)/shard_map/wave_1/ppermute | solution.py:60
  5.0 2.6 %collective-permute-start.1 = (bf16[160,512]{1,0:T(8,128)(2,1)S(1)}, bf16[160,512]{1,0:T(8,128)(2,1)S(1)}, u32[]{:S(2)}, u32[]{:S(2)}) collective-permute-start(bf16[160,512]{1,0:T(8,128)(2,1)S(1)} %get-tuple-element.60), channel_id=1, source_target_pairs={{0,8},{4,12},{8,0},{12,4},{1,9},{5,13},{9,1},{13,5},{2,10},{6,14},... | collective-permute-start | bytes 491528 | tf_op jit(solution)/shard_map/wave_2/ppermute | solution.py:60
  7.6 2.4 %prepare.2 = (bf16[160,512]{1,0:T(8,128)(2,1)S(1)}, bf16[160,512]{1,0:T(8,128)(2,1)S(1)}, bf16[160,512]{1,0:T(8,128)(2,1)S(1)}, bf16[160,512]{1,0:T(8,128)(2,1)S...) custom-call(s32[16]{0:T(128)} %owner_hbm.3, ...), custom_call_target="tpu_custom_call" | custom-call | flops 1 | bytes 1 | tf_op jit(solution)/shard_map/prepare/pallas_call | solution.py:141
  11.0 3.0 %collective-permute-start.6 = (bf16[160,512]{1,0:T(8,128)(2,1)S(1)}, bf16[160,512]{1,0:T(8,128)(2,1)S(1)}, u32[]{:S(2)}, u32[]{:S(2)}) collective-permute-start(bf16[160,512]{1,0:T(8,128)(2,1)S(1)} %get-tuple-element.69), channel_id=1, source_target_pairs={{0,12},{4,8},{8,4},{12,0},{1,13},{5,9},{9,5},{13,1},{2,14},{6,10},... | collective-permute-start | bytes 491528 | tf_op jit(solution)/shard_map/wave_3/ppermute | solution.py:60
  14.5 2.7 %turn.6.refs_0_ = bf16[1280,640]{1,0:T(8,128)(2,1)S(1)} custom-call(bf16[4,640,1280]{2,1,0:T(8,128)(2,1)} %table_hbm.3), custom_call_target="tpu_custom_call" | custom-call | flops 1 | bytes 1 | tf_op jit(solution)/shard_map/turn/pallas_call | solution.py:177
  17.2 2.7 %turn.4.refs_0_ = bf16[1280,640]{1,0:T(8,128)(2,1)S(1)} custom-call(bf16[4,640,1280]{2,1,0:T(8,128)(2,1)} %table_hbm.3), custom_call_target="tpu_custom_call" | custom-call | flops 1 | bytes 1 | tf_op jit(solution)/shard_map/turn/pallas_call | solution.py:177
  20.9 5.9 %collective-permute-done.6.refs_4_ = bf16[160,512]{1,0:T(8,128)(2,1)S(1)} collective-permute-done((bf16[160,512]{1,0:T(8,128)(2,1)S(1)}, bf16[160,512]{1,0:T(8,128)(2,1)S(1)}, u32[]{:S(2)}, u32[]{:S(2)}) %collective-permute-start.6) | collective-permute-done | bytes 163872 | tf_op jit(solution)/shard_map/wave_3/ppermute | solution.py:60
  26.8 9.5 %collective-permute-done.5.refs_3_ = bf16[160,512]{1,0:T(8,128)(2,1)S(1)} collective-permute-done((bf16[160,512]{1,0:T(8,128)(2,1)S(1)}, bf16[160,512]{1,0:T(8,128)(2,1)S(1)}, u32[]{:S(2)}, u32[]{:S(2)}) %collective-permute-start.5) | collective-permute-done | bytes 163872 | tf_op jit(solution)/shard_map/wave_2/ppermute | solution.py:60
  37.8 2.5 %collective-permute-start.12 = (bf16[160,512]{1,0:T(8,128)(2,1)S(1)}, bf16[160,512]{1,0:T(8,128)(2,1)S(1)}, u32[]{:S(2)}, u32[]{:S(2)}) collective-permute-start(bf16[160,512]{1,0:T(8,128)(2,1)S(1)} %get-tuple-element.79), channel_id=1, source_target_pairs={{0,12},{4,8},{8,4},{12,0},{1,13},{5,9},{9,5},{13,1},{2,14},{6,10},... | collective-permute-start | bytes 491528 | tf_op jit(solution)/shard_map/wave_3/ppermute | solution.py:60
  40.3 1.9 %collective-permute-start.10 = (bf16[160,512]{1,0:T(8,128)(2,1)S(1)}, bf16[160,512]{1,0:T(8,128)(2,1)S(1)}, u32[]{:S(2)}, u32[]{:S(2)}) collective-permute-start(bf16[160,512]{1,0:T(8,128)(2,1)S(1)} %get-tuple-element.75), channel_id=1, source_target_pairs={{0,4},{4,0},{8,12},{12,8},{1,5},{5,1},{9,13},{13,9},{2,6},{6,2},{1... | collective-permute-start | bytes 491528 | tf_op jit(solution)/shard_map/wave_1/ppermute | solution.py:60
  42.2 1.5 %collective-permute-start.9 = (bf16[320,512]{1,0:T(8,128)(2,1)S(1)}, bf16[320,512]{1,0:T(8,128)(2,1)S(1)}, u32[]{:S(2)}, u32[]{:S(2)}) collective-permute-start(bf16[320,512]{1,0:T(8,128)(2,1)S(1)} %combine.4), channel_id=1, source_target_pairs={{0,2},{1,3},{2,0},{3,1},{4,6},{5,7},{6,4},{7,5},{8,10},{9,11},{10,... | collective-permute-start | bytes 983048 | tf_op jit(solution)/shard_map/lat_2/ppermute | solution.py:60
  44.4 2.7 %turn.7.refs_0_ = bf16[1280,640]{1,0:T(8,128)(2,1)S(1)} custom-call(bf16[4,640,1280]{2,1,0:T(8,128)(2,1)} %table_hbm.3), custom_call_target="tpu_custom_call" | custom-call | flops 1 | bytes 1 | tf_op jit(solution)/shard_map/turn/pallas_call | solution.py:177
  47.1 2.7 %turn.5.refs_0_ = bf16[1280,640]{1,0:T(8,128)(2,1)S(1)} custom-call(bf16[4,640,1280]{2,1,0:T(8,128)(2,1)} %table_hbm.3), custom_call_target="tpu_custom_call" | custom-call | flops 1 | bytes 1 | tf_op jit(solution)/shard_map/turn/pallas_call | solution.py:177
  50.1 1.4 %collective-permute-done.9.far_ref = bf16[320,512]{1,0:T(8,128)(2,1)S(1)} collective-permute-done((bf16[320,512]{1,0:T(8,128)(2,1)S(1)}, bf16[320,512]{1,0:T(8,128)(2,1)S(1)}, u32[]{:S(2)}, u32[]{:S(2)}) %collective-permute-start.9) | collective-permute-done | bytes 327712 | tf_op jit(solution)/shard_map/lat_2/ppermute | solution.py:60
  51.5 2.5 %collective-permute-start.16 = (bf16[160,512]{1,0:T(8,128)(2,1)S(1)}, bf16[160,512]{1,0:T(8,128)(2,1)S(1)}, u32[]{:S(2)}, u32[]{:S(2)}) collective-permute-start(bf16[160,512]{1,0:T(8,128)(2,1)S(1)} %get-tuple-element.89), channel_id=1, source_target_pairs={{0,12},{4,8},{8,4},{12,0},{1,13},{5,9},{9,5},{13,1},{2,14},{6,10},... | collective-permute-start | bytes 491528 | tf_op jit(solution)/shard_map/wave_3/ppermute | solution.py:60
  55.1 1.6 %collective-permute-start.8 = (bf16[320,512]{1,0:T(8,128)(2,1)S(1)}, bf16[320,512]{1,0:T(8,128)(2,1)S(1)}, u32[]{:S(2)}, u32[]{:S(2)}) collective-permute-start(bf16[320,512]{1,0:T(8,128)(2,1)S(1)} %combine.5), channel_id=1, source_target_pairs={{0,2},{1,3},{2,0},{3,1},{4,6},{5,7},{6,4},{7,5},{8,10},{9,11},{10,... | collective-permute-start | bytes 983048 | tf_op jit(solution)/shard_map/lat_2/ppermute | solution.py:60
  58.0 1.4 %collective-permute-done.13.got_ref.near_ref = bf16[2,320,512]{2,1,0:T(8,128)(2,1)S(1)} collective-permute-done((bf16[2,320,512]{2,1,0:T(8,128)(2,1)S(1)}, bf16[2,320,512]{2,1,0:T(8,128)(2,1)S(1)}, u32[]{:S(2)}, u32[]{:S(2)}) %collective-permute-start.13) | collective-permute-done | bytes 655392 | tf_op jit(solution)/shard_map/lat_1/ppermute | solution.py:60
  60.1 4.3 %collective-permute-done.8.far_ref = bf16[320,512]{1,0:T(8,128)(2,1)S(1)} collective-permute-done((bf16[320,512]{1,0:T(8,128)(2,1)S(1)}, bf16[320,512]{1,0:T(8,128)(2,1)S(1)}, u32[]{:S(2)}, u32[]{:S(2)}) %collective-permute-start.8) | collective-permute-done | bytes 327712 | tf_op jit(solution)/shard_map/lat_2/ppermute | solution.py:60
  65.5 2.7 %collective-permute-done.15.refs_3_ = bf16[160,512]{1,0:T(8,128)(2,1)S(1)} collective-permute-done((bf16[160,512]{1,0:T(8,128)(2,1)S(1)}, bf16[160,512]{1,0:T(8,128)(2,1)S(1)}, u32[]{:S(2)}, u32[]{:S(2)}) %collective-permute-start.15) | collective-permute-done | bytes 163872 | tf_op jit(solution)/shard_map/wave_2/ppermute | solution.py:60
  69.6 1.4 %collective-permute-done.17.got_ref.near_ref = bf16[2,320,512]{2,1,0:T(8,128)(2,1)S(1)} collective-permute-done((bf16[2,320,512]{2,1,0:T(8,128)(2,1)S(1)}, bf16[2,320,512]{2,1,0:T(8,128)(2,1)S(1)}, u32[]{:S(2)}, u32[]{:S(2)}) %collective-permute-start.17) | collective-permute-done | bytes 655392 | tf_op jit(solution)/shard_map/lat_1/ppermute | solution.py:60
  71.0 1.6 %collective-permute-start.18 = (bf16[320,512]{1,0:T(8,128)(2,1)S(1)}, bf16[320,512]{1,0:T(8,128)(2,1)S(1)}, u32[]{:S(2)}, u32[]{:S(2)}) collective-permute-start(bf16[320,512]{1,0:T(8,128)(2,1)S(1)} %combine.7), channel_id=1, source_target_pairs={{0,2},{1,3},{2,0},{3,1},{4,6},{5,7},{6,4},{7,5},{8,10},{9,11},{10,... | collective-permute-start | bytes 983048 | tf_op jit(solution)/shard_map/lat_2/ppermute | solution.py:60
  72.6 1.0 %finish.6.refs_0_ = f32[320,2048]{1,0:T(8,128)} custom-call(s32[8,2048]{1,0:T(8,128)S(1)} %get-tuple-element.49.limit_ref, f32[2,320,512]{2,1,0:T(8,128)S(1)} %multiply_own.6.keep_ref, bf16[2,320,512]{2,1,0:T(8,128)(2,1)S(1)} %collective-permute-done.13.got_ref.near_ref, ...), custom_call_target="tpu_custom_call", output_to_operand_aliasing={{}: (4, {})} | custom-call | flops 1 | bytes 1 | tf_op jit(solution)/shard_map/finish/pallas_call | solution.py:254
  73.6 7.3 %collective-permute-done.18.far_ref = bf16[320,512]{1,0:T(8,128)(2,1)S(1)} collective-permute-done((bf16[320,512]{1,0:T(8,128)(2,1)S(1)}, bf16[320,512]{1,0:T(8,128)(2,1)S(1)}, u32[]{:S(2)}, u32[]{:S(2)}) %collective-permute-start.18) | collective-permute-done | bytes 327712 | tf_op jit(solution)/shard_map/lat_2/ppermute | solution.py:60
  (38 shorter events, 11.3 us)
Async XLA Ops:
  1.9 12.1 %collective-permute-start = (bf16[160,512]{1,0:T(8,128)(2,1)S(1)}, bf16[160,512]{1,0:T(8,128)(2,1)S(1)}, u32[]{:S(2)}, u32[]{:S(2)}) collective-permute-start(bf16[160,512]{1,0:T(8,128)(2,1)S(1)} %get-tuple-element.59), channel_id=1, source_target_pairs={{0,4},{4,0},{8,12},{12,8},{1,5},{5,1},{9,13},{13,9},{2,6},{6,2},{1... | collective-permute-start | bytes 491528 | tf_op jit(solution)/shard_map/wave_1/ppermute | solution.py:60
  5.0 15.1 %collective-permute-start.1 = (bf16[160,512]{1,0:T(8,128)(2,1)S(1)}, bf16[160,512]{1,0:T(8,128)(2,1)S(1)}, u32[]{:S(2)}, u32[]{:S(2)}) collective-permute-start(bf16[160,512]{1,0:T(8,128)(2,1)S(1)} %get-tuple-element.60), channel_id=1, source_target_pairs={{0,8},{4,12},{8,0},{12,4},{1,9},{5,13},{9,1},{13,5},{2,10},{6,14},... | collective-permute-start | bytes 491528 | tf_op jit(solution)/shard_map/wave_2/ppermute | solution.py:60
  7.6 12.5 %collective-permute-start.2 = (bf16[160,512]{1,0:T(8,128)(2,1)S(1)}, bf16[160,512]{1,0:T(8,128)(2,1)S(1)}, u32[]{:S(2)}, u32[]{:S(2)}) collective-permute-start(bf16[160,512]{1,0:T(8,128)(2,1)S(1)} %get-tuple-element.61), channel_id=1, source_target_pairs={{0,12},{4,8},{8,4},{12,0},{1,13},{5,9},{9,5},{13,1},{2,14},{6,10},... | collective-permute-start | bytes 491528 | tf_op jit(solution)/shard_map/wave_3/ppermute | solution.py:60
  10.1 10.8 %collective-permute-start.4 = (bf16[160,512]{1,0:T(8,128)(2,1)S(1)}, bf16[160,512]{1,0:T(8,128)(2,1)S(1)}, u32[]{:S(2)}, u32[]{:S(2)}) collective-permute-start(bf16[160,512]{1,0:T(8,128)(2,1)S(1)} %get-tuple-element.67), channel_id=1, source_target_pairs={{0,4},{4,0},{8,12},{12,8},{1,5},{5,1},{9,13},{13,9},{2,6},{6,2},{1... | collective-permute-start | bytes 491528 | tf_op jit(solution)/shard_map/wave_1/ppermute | solution.py:60
  11.0 15.7 %collective-permute-start.6 = (bf16[160,512]{1,0:T(8,128)(2,1)S(1)}, bf16[160,512]{1,0:T(8,128)(2,1)S(1)}, u32[]{:S(2)}, u32[]{:S(2)}) collective-permute-start(bf16[160,512]{1,0:T(8,128)(2,1)S(1)} %get-tuple-element.69), channel_id=1, source_target_pairs={{0,12},{4,8},{8,4},{12,0},{1,13},{5,9},{9,5},{13,1},{2,14},{6,10},... | collective-permute-start | bytes 491528 | tf_op jit(solution)/shard_map/wave_3/ppermute | solution.py:60
  14.0 22.2 %collective-permute-start.5 = (bf16[160,512]{1,0:T(8,128)(2,1)S(1)}, bf16[160,512]{1,0:T(8,128)(2,1)S(1)}, u32[]{:S(2)}, u32[]{:S(2)}) collective-permute-start(bf16[160,512]{1,0:T(8,128)(2,1)S(1)} %get-tuple-element.68), channel_id=1, source_target_pairs={{0,8},{4,12},{8,0},{12,4},{1,9},{5,13},{9,1},{13,5},{2,10},{6,14},... | collective-permute-start | bytes 491528 | tf_op jit(solution)/shard_map/wave_2/ppermute | solution.py:60
  20.8 16.9 %collective-permute-start.3 = (bf16[2,320,512]{2,1,0:T(8,128)(2,1)S(1)}, bf16[2,320,512]{2,1,0:T(8,128)(2,1)S(1)}, u32[]{:S(2)}, u32[]{:S(2)}) collective-permute-start(bf16[2,320,512]{2,1,0:T(8,128)(2,1)S(1)} %multiply_other.4), channel_id=1, source_target_pairs={{0,1},{1,0},{2,3},{3,2},{4,5},{5,4},{6,7},{7,6},{8,9},{9,8},{10,11... | collective-permute-start | bytes 1966088 | tf_op jit(solution)/shard_map/lat_1/ppermute | solution.py:60
  36.9 12.9 %collective-permute-start.7 = (bf16[2,320,512]{2,1,0:T(8,128)(2,1)S(1)}, bf16[2,320,512]{2,1,0:T(8,128)(2,1)S(1)}, u32[]{:S(2)}, u32[]{:S(2)}) collective-permute-start(bf16[2,320,512]{2,1,0:T(8,128)(2,1)S(1)} %multiply_other.5), channel_id=1, source_target_pairs={{0,1},{1,0},{2,3},{3,2},{4,5},{5,4},{6,7},{7,6},{8,9},{9,8},{10,11... | collective-permute-start | bytes 1966088 | tf_op jit(solution)/shard_map/lat_1/ppermute | solution.py:60
  37.8 17.2 %collective-permute-start.12 = (bf16[160,512]{1,0:T(8,128)(2,1)S(1)}, bf16[160,512]{1,0:T(8,128)(2,1)S(1)}, u32[]{:S(2)}, u32[]{:S(2)}) collective-permute-start(bf16[160,512]{1,0:T(8,128)(2,1)S(1)} %get-tuple-element.79), channel_id=1, source_target_pairs={{0,12},{4,8},{8,4},{12,0},{1,13},{5,9},{9,5},{13,1},{2,14},{6,10},... | collective-permute-start | bytes 491528 | tf_op jit(solution)/shard_map/wave_3/ppermute | solution.py:60
  40.3 14.7 %collective-permute-start.11 = (bf16[160,512]{1,0:T(8,128)(2,1)S(1)}, bf16[160,512]{1,0:T(8,128)(2,1)S(1)}, u32[]{:S(2)}, u32[]{:S(2)}) collective-permute-start(bf16[160,512]{1,0:T(8,128)(2,1)S(1)} %get-tuple-element.77), channel_id=1, source_target_pairs={{0,8},{4,12},{8,0},{12,4},{1,9},{5,13},{9,1},{13,5},{2,10},{6,14},... | collective-permute-start | bytes 491528 | tf_op jit(solution)/shard_map/wave_2/ppermute | solution.py:60
  40.3 16.3 %collective-permute-start.10 = (bf16[160,512]{1,0:T(8,128)(2,1)S(1)}, bf16[160,512]{1,0:T(8,128)(2,1)S(1)}, u32[]{:S(2)}, u32[]{:S(2)}) collective-permute-start(bf16[160,512]{1,0:T(8,128)(2,1)S(1)} %get-tuple-element.75), channel_id=1, source_target_pairs={{0,4},{4,0},{8,12},{12,8},{1,5},{5,1},{9,13},{13,9},{2,6},{6,2},{1... | collective-permute-start | bytes 491528 | tf_op jit(solution)/shard_map/wave_1/ppermute | solution.py:60
  42.2 9.3 %collective-permute-start.9 = (bf16[320,512]{1,0:T(8,128)(2,1)S(1)}, bf16[320,512]{1,0:T(8,128)(2,1)S(1)}, u32[]{:S(2)}, u32[]{:S(2)}) collective-permute-start(bf16[320,512]{1,0:T(8,128)(2,1)S(1)} %combine.4), channel_id=1, source_target_pairs={{0,2},{1,3},{2,0},{3,1},{4,6},{5,7},{6,4},{7,5},{8,10},{9,11},{10,... | collective-permute-start | bytes 983048 | tf_op jit(solution)/shard_map/lat_2/ppermute | solution.py:60
  49.8 15.6 %collective-permute-start.14 = (bf16[160,512]{1,0:T(8,128)(2,1)S(1)}, bf16[160,512]{1,0:T(8,128)(2,1)S(1)}, u32[]{:S(2)}, u32[]{:S(2)}) collective-permute-start(bf16[160,512]{1,0:T(8,128)(2,1)S(1)} %get-tuple-element.85), channel_id=1, source_target_pairs={{0,4},{4,0},{8,12},{12,8},{1,5},{5,1},{9,13},{13,9},{2,6},{6,2},{1... | collective-permute-start | bytes 491528 | tf_op jit(solution)/shard_map/wave_1/ppermute | solution.py:60
  51.5 14.0 %collective-permute-start.16 = (bf16[160,512]{1,0:T(8,128)(2,1)S(1)}, bf16[160,512]{1,0:T(8,128)(2,1)S(1)}, u32[]{:S(2)}, u32[]{:S(2)}) collective-permute-start(bf16[160,512]{1,0:T(8,128)(2,1)S(1)} %get-tuple-element.89), channel_id=1, source_target_pairs={{0,12},{4,8},{8,4},{12,0},{1,13},{5,9},{9,5},{13,1},{2,14},{6,10},... | collective-permute-start | bytes 491528 | tf_op jit(solution)/shard_map/wave_3/ppermute | solution.py:60
  55.0 13.2 %collective-permute-start.15 = (bf16[160,512]{1,0:T(8,128)(2,1)S(1)}, bf16[160,512]{1,0:T(8,128)(2,1)S(1)}, u32[]{:S(2)}, u32[]{:S(2)}) collective-permute-start(bf16[160,512]{1,0:T(8,128)(2,1)S(1)} %get-tuple-element.87), channel_id=1, source_target_pairs={{0,8},{4,12},{8,0},{12,4},{1,9},{5,13},{9,1},{13,5},{2,10},{6,14},... | collective-permute-start | bytes 491528 | tf_op jit(solution)/shard_map/wave_2/ppermute | solution.py:60
  55.1 9.4 %collective-permute-start.8 = (bf16[320,512]{1,0:T(8,128)(2,1)S(1)}, bf16[320,512]{1,0:T(8,128)(2,1)S(1)}, u32[]{:S(2)}, u32[]{:S(2)}) collective-permute-start(bf16[320,512]{1,0:T(8,128)(2,1)S(1)} %combine.5), channel_id=1, source_target_pairs={{0,2},{1,3},{2,0},{3,1},{4,6},{5,7},{6,4},{7,5},{8,10},{9,11},{10,... | collective-permute-start | bytes 983048 | tf_op jit(solution)/shard_map/lat_2/ppermute | solution.py:60
  57.3 2.2 %collective-permute-start.13 = (bf16[2,320,512]{2,1,0:T(8,128)(2,1)S(1)}, bf16[2,320,512]{2,1,0:T(8,128)(2,1)S(1)}, u32[]{:S(2)}, u32[]{:S(2)}) collective-permute-start(bf16[2,320,512]{2,1,0:T(8,128)(2,1)S(1)} %multiply_other.6), channel_id=1, source_target_pairs={{0,1},{1,0},{2,3},{3,2},{4,5},{5,4},{6,7},{7,6},{8,9},{9,8},{10,11... | collective-permute-start | bytes 1966088 | tf_op jit(solution)/shard_map/lat_1/ppermute | solution.py:60
  59.5 13.1 %collective-permute-start.19 = (bf16[320,512]{1,0:T(8,128)(2,1)S(1)}, bf16[320,512]{1,0:T(8,128)(2,1)S(1)}, u32[]{:S(2)}, u32[]{:S(2)}) collective-permute-start(bf16[320,512]{1,0:T(8,128)(2,1)S(1)} %combine.6), channel_id=1, source_target_pairs={{0,2},{1,3},{2,0},{3,1},{4,6},{5,7},{6,4},{7,5},{8,10},{9,11},{10,... | collective-permute-start | bytes 983048 | tf_op jit(solution)/shard_map/lat_2/ppermute | solution.py:60
  68.8 2.2 %collective-permute-start.17 = (bf16[2,320,512]{2,1,0:T(8,128)(2,1)S(1)}, bf16[2,320,512]{2,1,0:T(8,128)(2,1)S(1)}, u32[]{:S(2)}, u32[]{:S(2)}) collective-permute-start(bf16[2,320,512]{2,1,0:T(8,128)(2,1)S(1)} %multiply_other.7), channel_id=1, source_target_pairs={{0,1},{1,0},{2,3},{3,2},{4,5},{5,4},{6,7},{7,6},{8,9},{9,8},{10,11... | collective-permute-start | bytes 1966088 | tf_op jit(solution)/shard_map/lat_1/ppermute | solution.py:60
  71.0 9.8 %collective-permute-start.18 = (bf16[320,512]{1,0:T(8,128)(2,1)S(1)}, bf16[320,512]{1,0:T(8,128)(2,1)S(1)}, u32[]{:S(2)}, u32[]{:S(2)}) collective-permute-start(bf16[320,512]{1,0:T(8,128)(2,1)S(1)} %combine.7), channel_id=1, source_target_pairs={{0,2},{1,3},{2,0},{3,1},{4,6},{5,7},{6,4},{7,5},{8,10},{9,11},{10,... | collective-permute-start | bytes 983048 | tf_op jit(solution)/shard_map/lat_2/ppermute | solution.py:60

commit v4 on v3

--- a/solution.py
+++ b/solution.py
@@ -13,9 +13,9 @@
 LARGE = pl.CostEstimate(flops=1, transcendentals=0, bytes_accessed=1)
 HUGE = pl.CostEstimate(flops=20000000000, transcendentals=0, bytes_accessed=1)
 SMALL = pl.CostEstimate(flops=1, transcendentals=0, bytes_accessed=1)
-WINDOW = 6
+WINDOW = 7
 EARLY = 2
-PINS = ('sent', 'none', 'none', 'none')
+PINS = ('sent', 'none', 'sent', 'none')
 OUTS = 1
 SEQ = (1, 1, 1, 1, 1)
 CLOSE = 1
@@ -344,7 +344,7 @@
         if at >= 2 and OUTS:
             held.tie(("row", at, 0), "out")
         if at >= 1 and SEQ[at - 1]:
-            held.tie(("row", at, 0), ("sent", at - 1))
+            held.tie(("row", at, 0), ("keep", at - 1), ("near", at - 1))
         multiply_other(at)
         hold(at, "other")
         pass_core(at)

time: 82.2 us -> 79 us (0.961)
  waiting for transfers between devices: 34 us -> 28.1 us
  starting transfers between devices: 22.8 us -> 24.9 us
    ppermute x20, waiting for transfers between devices: 34 us -> 28.1 us  [exchange(): return lax.ppermute(value, axis, [(i, i ^ step) for i in range(size)])]
    ppermute x20, starting transfers between devices: 22.8 us -> 24.9 us  [exchange(): return lax.ppermute(value, axis, [(i, i ^ step) for i in range(size)])]
  transfers between devices with their start and end apart: 20 -> 20, of which waited for: 9 -> 11; matrix products, arithmetic and copies ran while one was open for 0% -> 0% of each run, Pallas kernels for 27% -> 27%
where the time goes in v4:
time: 79 us; the launch traced here: 78 us
  waiting for transfers between devices  28.1 us (36%)
  starting transfers between devices  24.9 us (32%)
  Pallas kernels  24.7 us (31%)
    ppermute x20, waiting for transfers between devices, exchange(): return lax.ppermute(value, axis, [(i, i ^ step) for i in range(size)])  28.1 us
    ppermute x20, starting transfers between devices, exchange(): return lax.ppermute(value, axis, [(i, i ^ step) for i in range(size)])  24.9 us
    pallas_call x4, Pallas kernels, turn(): pl.pallas_call(functools.partial(turn_body, slot, rows), in_specs=[pl.Blo...  10.8 us
    pallas_call x8, Pallas kernels, multiply(): pl.pallas_call(functools.partial(multiply_body, other, parts), in_specs=[...  5.34 us
    pallas_call x2, Pallas kernels, prepare(): pl.pallas_call(functools.partial(prepare_body, stride, own_slots, chunks,...  4.37 us
    pallas_call x4, Pallas kernels, finish(): pl.pallas_call(functools.partial(finish_body, first), in_specs=[WHOLE] *...  3.95 us
  transfers between devices with their start and end apart: 20, of which 11 were waited for; matrix products, arithmetic and copies ran while one was open for 0% of the time, Pallas kernels for 27%

profile of v4, /device:TPU:0, one launch (start us, length us, event | category | flops | bytes accessed | tf_op | source)
XLA Modules:
  0.0 78.0 jit_solution(12001099885917573542)
XLA Ops:
  0.0 1.9 %prepare.3 = (bf16[160,512]{1,0:T(8,128)(2,1)S(1)}, bf16[160,512]{1,0:T(8,128)(2,1)S(1)}, bf16[160,512]{1,0:T(8,128)(2,1)S(1)}, bf16[160,512]{1,0:T(8,128)(2,1)S(1)}) custom-call(s32[16]{0:T(128)} %owner_hbm.3, f32[640]{0:T(1024)} %gauss_hbm.3, s32[160]{0:T(256)} %points_hbm.3, bf16[160,8192]{1,0:T(8,128)(2,1)} %source.3), custom_call_target="tpu_custom_call" | custom-call | flops 1 | bytes 1 | tf_op jit(solution)/shard_map/prepare/pallas_call | solution.py:141
  1.9 3.1 %collective-permute-start = (bf16[160,512]{1,0:T(8,128)(2,1)S(1)}, bf16[160,512]{1,0:T(8,128)(2,1)S(1)}, u32[]{:S(2)}, u32[]{:S(2)}) collective-permute-start(bf16[160,512]{1,0:T(8,128)(2,1)S(1)} %get-tuple-element.67), channel_id=1, source_target_pairs={{0,4},{4,0},{8,12},{12,8},{1,5},{5,1},{9,13},{13,9},{2,6},{6,2},{1... | collective-permute-start | bytes 491528 | tf_op jit(solution)/shard_map/wave_1/ppermute | solution.py:60
  5.0 2.6 %collective-permute-start.1 = (bf16[160,512]{1,0:T(8,128)(2,1)S(1)}, bf16[160,512]{1,0:T(8,128)(2,1)S(1)}, u32[]{:S(2)}, u32[]{:S(2)}) collective-permute-start(bf16[160,512]{1,0:T(8,128)(2,1)S(1)} %get-tuple-element.68), channel_id=1, source_target_pairs={{0,8},{4,12},{8,0},{12,4},{1,9},{5,13},{9,1},{13,5},{2,10},{6,14},... | collective-permute-start | bytes 491528 | tf_op jit(solution)/shard_map/wave_2/ppermute | solution.py:60
  7.6 2.4 %prepare.2 = (bf16[160,512]{1,0:T(8,128)(2,1)S(1)}, bf16[160,512]{1,0:T(8,128)(2,1)S(1)}, bf16[160,512]{1,0:T(8,128)(2,1)S(1)}, bf16[160,512]{1,0:T(8,128)(2,1)S...) custom-call(s32[16]{0:T(128)} %owner_hbm.3, ...), custom_call_target="tpu_custom_call" | custom-call | flops 1 | bytes 1 | tf_op jit(solution)/shard_map/prepare/pallas_call | solution.py:141
  11.0 3.0 %collective-permute-start.7 = (bf16[160,512]{1,0:T(8,128)(2,1)S(1)}, bf16[160,512]{1,0:T(8,128)(2,1)S(1)}, u32[]{:S(2)}, u32[]{:S(2)}) collective-permute-start(bf16[160,512]{1,0:T(8,128)(2,1)S(1)} %get-tuple-element.81), channel_id=1, source_target_pairs={{0,12},{4,8},{8,4},{12,0},{1,13},{5,9},{9,5},{13,1},{2,14},{6,10},... | collective-permute-start | bytes 491528 | tf_op jit(solution)/shard_map/wave_3/ppermute | solution.py:60
  14.0 2.7 %turn.6.refs_0_ = bf16[1280,640]{1,0:T(8,128)(2,1)S(1)} custom-call(bf16[4,640,1280]{2,1,0:T(8,128)(2,1)} %table_hbm.3), custom_call_target="tpu_custom_call" | custom-call | flops 1 | bytes 1 | tf_op jit(solution)/shard_map/turn/pallas_call | solution.py:177
  16.7 2.7 %turn.4.refs_0_ = bf16[1280,640]{1,0:T(8,128)(2,1)S(1)} custom-call(bf16[4,640,1280]{2,1,0:T(8,128)(2,1)} %table_hbm.3), custom_call_target="tpu_custom_call" | custom-call | flops 1 | bytes 1 | tf_op jit(solution)/shard_map/turn/pallas_call | solution.py:177
  21.5 5.2 %collective-permute-done.7.refs_4_ = bf16[160,512]{1,0:T(8,128)(2,1)S(1)} collective-permute-done((bf16[160,512]{1,0:T(8,128)(2,1)S(1)}, bf16[160,512]{1,0:T(8,128)(2,1)S(1)}, u32[]{:S(2)}, u32[]{:S(2)}) %collective-permute-start.7) | collective-permute-done | bytes 163872 | tf_op jit(solution)/shard_map/wave_3/ppermute | solution.py:60
  26.8 9.5 %collective-permute-done.6.refs_3_ = bf16[160,512]{1,0:T(8,128)(2,1)S(1)} collective-permute-done((bf16[160,512]{1,0:T(8,128)(2,1)S(1)}, bf16[160,512]{1,0:T(8,128)(2,1)S(1)}, u32[]{:S(2)}, u32[]{:S(2)}) %collective-permute-start.6) | collective-permute-done | bytes 163872 | tf_op jit(solution)/shard_map/wave_2/ppermute | solution.py:60
  37.1 2.5 %collective-permute-start.12 = (bf16[160,512]{1,0:T(8,128)(2,1)S(1)}, bf16[160,512]{1,0:T(8,128)(2,1)S(1)}, u32[]{:S(2)}, u32[]{:S(2)}) collective-permute-start(bf16[160,512]{1,0:T(8,128)(2,1)S(1)} %get-tuple-element.92), channel_id=1, source_target_pairs={{0,12},{4,8},{8,4},{12,0},{1,13},{5,9},{9,5},{13,1},{2,14},{6,10},... | collective-permute-start | bytes 491528 | tf_op jit(solution)/shard_map/wave_3/ppermute | solution.py:60
  39.6 1.9 %collective-permute-start.11 = (bf16[160,512]{1,0:T(8,128)(2,1)S(1)}, bf16[160,512]{1,0:T(8,128)(2,1)S(1)}, u32[]{:S(2)}, u32[]{:S(2)}) collective-permute-start(bf16[160,512]{1,0:T(8,128)(2,1)S(1)} %get-tuple-element.90), channel_id=1, source_target_pairs={{0,8},{4,12},{8,0},{12,4},{1,9},{5,13},{9,1},{13,5},{2,10},{6,14},... | collective-permute-start | bytes 491528 | tf_op jit(solution)/shard_map/wave_2/ppermute | solution.py:60
  41.5 1.5 %collective-permute-start.4 = (bf16[320,512]{1,0:T(8,128)(2,1)S(1)}, bf16[320,512]{1,0:T(8,128)(2,1)S(1)}, u32[]{:S(2)}, u32[]{:S(2)}) collective-permute-start(bf16[320,512]{1,0:T(8,128)(2,1)S(1)} %combine.4), channel_id=1, source_target_pairs={{0,2},{1,3},{2,0},{3,1},{4,6},{5,7},{6,4},{7,5},{8,10},{9,11},{10,... | collective-permute-start | bytes 983048 | tf_op jit(solution)/shard_map/lat_2/ppermute | solution.py:60
  43.7 2.7 %turn.7.refs_0_ = bf16[1280,640]{1,0:T(8,128)(2,1)S(1)} custom-call(bf16[4,640,1280]{2,1,0:T(8,128)(2,1)} %table_hbm.3), custom_call_target="tpu_custom_call" | custom-call | flops 1 | bytes 1 | tf_op jit(solution)/shard_map/turn/pallas_call | solution.py:177
  46.4 2.7 %turn.5.refs_0_ = bf16[1280,640]{1,0:T(8,128)(2,1)S(1)} custom-call(bf16[4,640,1280]{2,1,0:T(8,128)(2,1)} %table_hbm.3), custom_call_target="tpu_custom_call" | custom-call | flops 1 | bytes 1 | tf_op jit(solution)/shard_map/turn/pallas_call | solution.py:177
  50.8 1.6 %collective-permute-start.14 = (bf16[160,512]{1,0:T(8,128)(2,1)S(1)}, bf16[160,512]{1,0:T(8,128)(2,1)S(1)}, u32[]{:S(2)}, u32[]{:S(2)}) collective-permute-start(bf16[160,512]{1,0:T(8,128)(2,1)S(1)} %get-tuple-element.99), channel_id=1, source_target_pairs={{0,4},{4,0},{8,12},{12,8},{1,5},{5,1},{9,13},{13,9},{2,6},{6,2},{1... | collective-permute-start | bytes 491528 | tf_op jit(solution)/shard_map/wave_1/ppermute | solution.py:60
  53.4 1.4 %collective-permute-start.16 = (bf16[160,512]{1,0:T(8,128)(2,1)S(1)}, bf16[160,512]{1,0:T(8,128)(2,1)S(1)}, u32[]{:S(2)}, u32[]{:S(2)}) collective-permute-start(bf16[160,512]{1,0:T(8,128)(2,1)S(1)} %get-tuple-element.103), channel_id=1, source_target_pairs={{0,12},{4,8},{8,4},{12,0},{1,13},{5,9},{9,5},{13,1},{2,14},{6,10},... | collective-permute-start | bytes 491528 | tf_op jit(solution)/shard_map/wave_3/ppermute | solution.py:60
  54.8 1.3 %collective-permute-start.9 = (bf16[320,512]{1,0:T(8,128)(2,1)S(1)}, bf16[320,512]{1,0:T(8,128)(2,1)S(1)}, u32[]{:S(2)}, u32[]{:S(2)}) collective-permute-start(bf16[320,512]{1,0:T(8,128)(2,1)S(1)} %combine.5), channel_id=1, source_target_pairs={{0,2},{1,3},{2,0},{3,1},{4,6},{5,7},{6,4},{7,5},{8,10},{9,11},{10,... | collective-permute-start | bytes 983048 | tf_op jit(solution)/shard_map/lat_2/ppermute | solution.py:60
  58.7 1.4 %collective-permute-done.13.got_ref.near_ref = bf16[2,320,512]{2,1,0:T(8,128)(2,1)S(1)} collective-permute-done((bf16[2,320,512]{2,1,0:T(8,128)(2,1)S(1)}, bf16[2,320,512]{2,1,0:T(8,128)(2,1)S(1)}, u32[]{:S(2)}, u32[]{:S(2)}) %collective-permute-start.13) | collective-permute-done | bytes 655392 | tf_op jit(solution)/shard_map/lat_1/ppermute | solution.py:60
  60.2 1.6 %collective-permute-start.19 = (bf16[320,512]{1,0:T(8,128)(2,1)S(1)}, bf16[320,512]{1,0:T(8,128)(2,1)S(1)}, u32[]{:S(2)}, u32[]{:S(2)}) collective-permute-start(bf16[320,512]{1,0:T(8,128)(2,1)S(1)} %combine.6), channel_id=1, source_target_pairs={{0,2},{1,3},{2,0},{3,1},{4,6},{5,7},{6,4},{7,5},{8,10},{9,11},{10,... | collective-permute-start | bytes 983048 | tf_op jit(solution)/shard_map/lat_2/ppermute | solution.py:60
  61.8 1.2 %collective-permute-done.9.far_ref = bf16[320,512]{1,0:T(8,128)(2,1)S(1)} collective-permute-done((bf16[320,512]{1,0:T(8,128)(2,1)S(1)}, bf16[320,512]{1,0:T(8,128)(2,1)S(1)}, u32[]{:S(2)}, u32[]{:S(2)}) %collective-permute-start.9) | collective-permute-done | bytes 327712 | tf_op jit(solution)/shard_map/lat_2/ppermute | solution.py:60
  65.8 1.4 %collective-permute-done.17.got_ref.near_ref = bf16[2,320,512]{2,1,0:T(8,128)(2,1)S(1)} collective-permute-done((bf16[2,320,512]{2,1,0:T(8,128)(2,1)S(1)}, bf16[2,320,512]{2,1,0:T(8,128)(2,1)S(1)}, u32[]{:S(2)}, u32[]{:S(2)}) %collective-permute-start.17) | collective-permute-done | bytes 655392 | tf_op jit(solution)/shard_map/lat_1/ppermute | solution.py:60
  67.2 1.6 %collective-permute-start.18 = (bf16[320,512]{1,0:T(8,128)(2,1)S(1)}, bf16[320,512]{1,0:T(8,128)(2,1)S(1)}, u32[]{:S(2)}, u32[]{:S(2)}) collective-permute-start(bf16[320,512]{1,0:T(8,128)(2,1)S(1)} %combine.7), channel_id=1, source_target_pairs={{0,2},{1,3},{2,0},{3,1},{4,6},{5,7},{6,4},{7,5},{8,10},{9,11},{10,... | collective-permute-start | bytes 983048 | tf_op jit(solution)/shard_map/lat_2/ppermute | solution.py:60
  68.8 1.2 %collective-permute-done.19.far_ref = bf16[320,512]{1,0:T(8,128)(2,1)S(1)} collective-permute-done((bf16[320,512]{1,0:T(8,128)(2,1)S(1)}, bf16[320,512]{1,0:T(8,128)(2,1)S(1)}, u32[]{:S(2)}, u32[]{:S(2)}) %collective-permute-start.19) | collective-permute-done | bytes 327712 | tf_op jit(solution)/shard_map/lat_2/ppermute | solution.py:60
  71.0 6.0 %collective-permute-done.18.far_ref = bf16[320,512]{1,0:T(8,128)(2,1)S(1)} collective-permute-done((bf16[320,512]{1,0:T(8,128)(2,1)S(1)}, bf16[320,512]{1,0:T(8,128)(2,1)S(1)}, u32[]{:S(2)}, u32[]{:S(2)}) %collective-permute-start.18) | collective-permute-done | bytes 327712 | tf_op jit(solution)/shard_map/lat_2/ppermute | solution.py:60
  (38 shorter events, 14.6 us)
Async XLA Ops:
  1.9 17.5 %collective-permute-start = (bf16[160,512]{1,0:T(8,128)(2,1)S(1)}, bf16[160,512]{1,0:T(8,128)(2,1)S(1)}, u32[]{:S(2)}, u32[]{:S(2)}) collective-permute-start(bf16[160,512]{1,0:T(8,128)(2,1)S(1)} %get-tuple-element.67), channel_id=1, source_target_pairs={{0,4},{4,0},{8,12},{12,8},{1,5},{5,1},{9,13},{13,9},{2,6},{6,2},{1... | collective-permute-start | bytes 491528 | tf_op jit(solution)/shard_map/wave_1/ppermute | solution.py:60
  5.0 15.1 %collective-permute-start.1 = (bf16[160,512]{1,0:T(8,128)(2,1)S(1)}, bf16[160,512]{1,0:T(8,128)(2,1)S(1)}, u32[]{:S(2)}, u32[]{:S(2)}) collective-permute-start(bf16[160,512]{1,0:T(8,128)(2,1)S(1)} %get-tuple-element.68), channel_id=1, source_target_pairs={{0,8},{4,12},{8,0},{12,4},{1,9},{5,13},{9,1},{13,5},{2,10},{6,14},... | collective-permute-start | bytes 491528 | tf_op jit(solution)/shard_map/wave_2/ppermute | solution.py:60
  7.6 12.5 %collective-permute-start.2 = (bf16[160,512]{1,0:T(8,128)(2,1)S(1)}, bf16[160,512]{1,0:T(8,128)(2,1)S(1)}, u32[]{:S(2)}, u32[]{:S(2)}) collective-permute-start(bf16[160,512]{1,0:T(8,128)(2,1)S(1)} %get-tuple-element.69), channel_id=1, source_target_pairs={{0,12},{4,8},{8,4},{12,0},{1,13},{5,9},{9,5},{13,1},{2,14},{6,10},... | collective-permute-start | bytes 491528 | tf_op jit(solution)/shard_map/wave_3/ppermute | solution.py:60
  10.1 26.2 %collective-permute-start.5 = (bf16[160,512]{1,0:T(8,128)(2,1)S(1)}, bf16[160,512]{1,0:T(8,128)(2,1)S(1)}, u32[]{:S(2)}, u32[]{:S(2)}) collective-permute-start(bf16[160,512]{1,0:T(8,128)(2,1)S(1)} %get-tuple-element.79), channel_id=1, source_target_pairs={{0,4},{4,0},{8,12},{12,8},{1,5},{5,1},{9,13},{13,9},{2,6},{6,2},{1... | collective-permute-start | bytes 491528 | tf_op jit(solution)/shard_map/wave_1/ppermute | solution.py:60
  11.0 15.7 %collective-permute-start.7 = (bf16[160,512]{1,0:T(8,128)(2,1)S(1)}, bf16[160,512]{1,0:T(8,128)(2,1)S(1)}, u32[]{:S(2)}, u32[]{:S(2)}) collective-permute-start(bf16[160,512]{1,0:T(8,128)(2,1)S(1)} %get-tuple-element.81), channel_id=1, source_target_pairs={{0,12},{4,8},{8,4},{12,0},{1,13},{5,9},{9,5},{13,1},{2,14},{6,10},... | collective-permute-start | bytes 491528 | tf_op jit(solution)/shard_map/wave_3/ppermute | solution.py:60
  19.5 16.8 %collective-permute-start.6 = (bf16[160,512]{1,0:T(8,128)(2,1)S(1)}, bf16[160,512]{1,0:T(8,128)(2,1)S(1)}, u32[]{:S(2)}, u32[]{:S(2)}) collective-permute-start(bf16[160,512]{1,0:T(8,128)(2,1)S(1)} %get-tuple-element.80), channel_id=1, source_target_pairs={{0,8},{4,12},{8,0},{12,4},{1,9},{5,13},{9,1},{13,5},{2,10},{6,14},... | collective-permute-start | bytes 491528 | tf_op jit(solution)/shard_map/wave_2/ppermute | solution.py:60
  20.8 15.5 %collective-permute-start.3 = (bf16[2,320,512]{2,1,0:T(8,128)(2,1)S(1)}, bf16[2,320,512]{2,1,0:T(8,128)(2,1)S(1)}, u32[]{:S(2)}, u32[]{:S(2)}) collective-permute-start(bf16[2,320,512]{2,1,0:T(8,128)(2,1)S(1)} %multiply_other.4), channel_id=1, source_target_pairs={{0,1},{1,0},{2,3},{3,2},{4,5},{5,4},{6,7},{7,6},{8,9},{9,8},{10,11... | collective-permute-start | bytes 1966088 | tf_op jit(solution)/shard_map/lat_1/ppermute | solution.py:60
  36.9 12.2 %collective-permute-start.8 = (bf16[2,320,512]{2,1,0:T(8,128)(2,1)S(1)}, bf16[2,320,512]{2,1,0:T(8,128)(2,1)S(1)}, u32[]{:S(2)}, u32[]{:S(2)}) collective-permute-start(bf16[2,320,512]{2,1,0:T(8,128)(2,1)S(1)} %multiply_other.5), channel_id=1, source_target_pairs={{0,1},{1,0},{2,3},{3,2},{4,5},{5,4},{6,7},{7,6},{8,9},{9,8},{10,11... | collective-permute-start | bytes 1966088 | tf_op jit(solution)/shard_map/lat_1/ppermute | solution.py:60
  37.1 16.3 %collective-permute-start.12 = (bf16[160,512]{1,0:T(8,128)(2,1)S(1)}, bf16[160,512]{1,0:T(8,128)(2,1)S(1)}, u32[]{:S(2)}, u32[]{:S(2)}) collective-permute-start(bf16[160,512]{1,0:T(8,128)(2,1)S(1)} %get-tuple-element.92), channel_id=1, source_target_pairs={{0,12},{4,8},{8,4},{12,0},{1,13},{5,9},{9,5},{13,1},{2,14},{6,10},... | collective-permute-start | bytes 491528 | tf_op jit(solution)/shard_map/wave_3/ppermute | solution.py:60
  39.6 15.2 %collective-permute-start.10 = (bf16[160,512]{1,0:T(8,128)(2,1)S(1)}, bf16[160,512]{1,0:T(8,128)(2,1)S(1)}, u32[]{:S(2)}, u32[]{:S(2)}) collective-permute-start(bf16[160,512]{1,0:T(8,128)(2,1)S(1)} %get-tuple-element.89), channel_id=1, source_target_pairs={{0,4},{4,0},{8,12},{12,8},{1,5},{5,1},{9,13},{13,9},{2,6},{6,2},{1... | collective-permute-start | bytes 491528 | tf_op jit(solution)/shard_map/wave_1/ppermute | solution.py:60
  39.6 17.7 %collective-permute-start.11 = (bf16[160,512]{1,0:T(8,128)(2,1)S(1)}, bf16[160,512]{1,0:T(8,128)(2,1)S(1)}, u32[]{:S(2)}, u32[]{:S(2)}) collective-permute-start(bf16[160,512]{1,0:T(8,128)(2,1)S(1)} %get-tuple-element.90), channel_id=1, source_target_pairs={{0,8},{4,12},{8,0},{12,4},{1,9},{5,13},{9,1},{13,5},{2,10},{6,14},... | collective-permute-start | bytes 491528 | tf_op jit(solution)/shard_map/wave_2/ppermute | solution.py:60
  41.5 9.3 %collective-permute-start.4 = (bf16[320,512]{1,0:T(8,128)(2,1)S(1)}, bf16[320,512]{1,0:T(8,128)(2,1)S(1)}, u32[]{:S(2)}, u32[]{:S(2)}) collective-permute-start(bf16[320,512]{1,0:T(8,128)(2,1)S(1)} %combine.4), channel_id=1, source_target_pairs={{0,2},{1,3},{2,0},{3,1},{4,6},{5,7},{6,4},{7,5},{8,10},{9,11},{10,... | collective-permute-start | bytes 983048 | tf_op jit(solution)/shard_map/lat_2/ppermute | solution.py:60
  49.1 15.2 %collective-permute-start.15 = (bf16[160,512]{1,0:T(8,128)(2,1)S(1)}, bf16[160,512]{1,0:T(8,128)(2,1)S(1)}, u32[]{:S(2)}, u32[]{:S(2)}) collective-permute-start(bf16[160,512]{1,0:T(8,128)(2,1)S(1)} %get-tuple-element.101), channel_id=1, source_target_pairs={{0,8},{4,12},{8,0},{12,4},{1,9},{5,13},{9,1},{13,5},{2,10},{6,14},... | collective-permute-start | bytes 491528 | tf_op jit(solution)/shard_map/wave_2/ppermute | solution.py:60
  50.8 13.5 %collective-permute-start.14 = (bf16[160,512]{1,0:T(8,128)(2,1)S(1)}, bf16[160,512]{1,0:T(8,128)(2,1)S(1)}, u32[]{:S(2)}, u32[]{:S(2)}) collective-permute-start(bf16[160,512]{1,0:T(8,128)(2,1)S(1)} %get-tuple-element.99), channel_id=1, source_target_pairs={{0,4},{4,0},{8,12},{12,8},{1,5},{5,1},{9,13},{13,9},{2,6},{6,2},{1... | collective-permute-start | bytes 491528 | tf_op jit(solution)/shard_map/wave_1/ppermute | solution.py:60
  53.4 10.9 %collective-permute-start.16 = (bf16[160,512]{1,0:T(8,128)(2,1)S(1)}, bf16[160,512]{1,0:T(8,128)(2,1)S(1)}, u32[]{:S(2)}, u32[]{:S(2)}) collective-permute-start(bf16[160,512]{1,0:T(8,128)(2,1)S(1)} %get-tuple-element.103), channel_id=1, source_target_pairs={{0,12},{4,8},{8,4},{12,0},{1,13},{5,9},{9,5},{13,1},{2,14},{6,10},... | collective-permute-start | bytes 491528 | tf_op jit(solution)/shard_map/wave_3/ppermute | solution.py:60
  54.8 8.1 %collective-permute-start.9 = (bf16[320,512]{1,0:T(8,128)(2,1)S(1)}, bf16[320,512]{1,0:T(8,128)(2,1)S(1)}, u32[]{:S(2)}, u32[]{:S(2)}) collective-permute-start(bf16[320,512]{1,0:T(8,128)(2,1)S(1)} %combine.5), channel_id=1, source_target_pairs={{0,2},{1,3},{2,0},{3,1},{4,6},{5,7},{6,4},{7,5},{8,10},{9,11},{10,... | collective-permute-start | bytes 983048 | tf_op jit(solution)/shard_map/lat_2/ppermute | solution.py:60
  58.0 2.2 %collective-permute-start.13 = (bf16[2,320,512]{2,1,0:T(8,128)(2,1)S(1)}, bf16[2,320,512]{2,1,0:T(8,128)(2,1)S(1)}, u32[]{:S(2)}, u32[]{:S(2)}) collective-permute-start(bf16[2,320,512]{2,1,0:T(8,128)(2,1)S(1)} %multiply_other.6), channel_id=1, source_target_pairs={{0,1},{1,0},{2,3},{3,2},{4,5},{5,4},{6,7},{7,6},{8,9},{9,8},{10,11... | collective-permute-start | bytes 1966088 | tf_op jit(solution)/shard_map/lat_1/ppermute | solution.py:60
  60.2 9.8 %collective-permute-start.19 = (bf16[320,512]{1,0:T(8,128)(2,1)S(1)}, bf16[320,512]{1,0:T(8,128)(2,1)S(1)}, u32[]{:S(2)}, u32[]{:S(2)}) collective-permute-start(bf16[320,512]{1,0:T(8,128)(2,1)S(1)} %combine.6), channel_id=1, source_target_pairs={{0,2},{1,3},{2,0},{3,1},{4,6},{5,7},{6,4},{7,5},{8,10},{9,11},{10,... | collective-permute-start | bytes 983048 | tf_op jit(solution)/shard_map/lat_2/ppermute | solution.py:60
  65.0 2.2 %collective-permute-start.17 = (bf16[2,320,512]{2,1,0:T(8,128)(2,1)S(1)}, bf16[2,320,512]{2,1,0:T(8,128)(2,1)S(1)}, u32[]{:S(2)}, u32[]{:S(2)}) collective-permute-start(bf16[2,320,512]{2,1,0:T(8,128)(2,1)S(1)} %multiply_other.7), channel_id=1, source_target_pairs={{0,1},{1,0},{2,3},{3,2},{4,5},{5,4},{6,7},{7,6},{8,9},{9,8},{10,11... | collective-permute-start | bytes 1966088 | tf_op jit(solution)/shard_map/lat_1/ppermute | solution.py:60
  67.2 9.8 %collective-permute-start.18 = (bf16[320,512]{1,0:T(8,128)(2,1)S(1)}, bf16[320,512]{1,0:T(8,128)(2,1)S(1)}, u32[]{:S(2)}, u32[]{:S(2)}) collective-permute-start(bf16[320,512]{1,0:T(8,128)(2,1)S(1)} %combine.7), channel_id=1, source_target_pairs={{0,2},{1,3},{2,0},{3,1},{4,6},{5,7},{6,4},{7,5},{8,10},{9,11},{10,... | collective-permute-start | bytes 983048 | tf_op jit(solution)/shard_map/lat_2/ppermute | solution.py:60

commit v5 on v4

--- a/solution.py
+++ b/solution.py
@@ -239,12 +239,21 @@
     share, width = total_ref.shape
     lat = lax.axis_index("lat")
     far = lat >> 1
-    degree = lat * share + lax.broadcasted_iota(jnp.int32, (share, width), 0)
-    total = keep_ref[far] + near_ref[far].astype(jnp.float32) + far_ref[...].astype(jnp.float32)
-    total_ref[...] = jnp.where(degree >= limit_ref[0:1, first : first + width], total, 0.0)
-    copy = pltpu.make_async_copy(total_ref, out_ref.at[:, first : first + width], sem)
-    copy.start()
-    copy.wait()
+    part = share // 4
+    copies = []
+    for at in range(4):
+        rows = slice(at * part, (at + 1) * part)
+        degree = lat * share + at * part + lax.broadcasted_iota(jnp.int32, (part, width), 0)
+        total = keep_ref[far, rows, :] + near_ref[far, rows, :].astype(jnp.float32)
+        total = total + far_ref[rows, :].astype(jnp.float32)
+        total_ref[rows, :] = jnp.where(degree >= limit_ref[0:1, first : first + width], total, 0.0)
+        copy = pltpu.make_async_copy(
+            total_ref.at[rows, :], out_ref.at[rows, first : first + width], sem.at[at]
+        )
+        copy.start()
+        copies.append(copy)
+    for copy in copies:
+        copy.wait()
 
 
 def finish(limits, keep, near, far, before, first):
@@ -257,7 +266,7 @@
         out_specs=hbm,
         out_shape=pltpu.HBM((share, limits.shape[1]), jnp.float32),
         input_output_aliases={4: 0} if old else {},
-        scratch_shapes=[pltpu.VMEM((share, width), jnp.float32), pltpu.SemaphoreType.DMA],
+        scratch_shapes=[pltpu.VMEM((share, width), jnp.float32), pltpu.SemaphoreType.DMA((4,))],
         compiler_params=PARAMS,
         cost_estimate=SMALL,
         name="finish",

time: 79 us -> 78.9 us (level)
  no operation moved by 1% of the time
where the time goes in v5:
time: 78.9 us; the launch traced here: 77.9 us
  waiting for transfers between devices  28.4 us (36%)
  starting transfers between devices  24.9 us (32%)
  Pallas kernels  24.4 us (31%)
    ppermute x20, waiting for transfers between devices, exchange(): return lax.ppermute(value, axis, [(i, i ^ step) for i in range(size)])  28.4 us
    ppermute x20, starting transfers between devices, exchange(): return lax.ppermute(value, axis, [(i, i ^ step) for i in range(size)])  24.9 us
    pallas_call x4, Pallas kernels, turn(): pl.pallas_call(functools.partial(turn_body, slot, rows), in_specs=[pl.Blo...  10.8 us
    pallas_call x8, Pallas kernels, multiply(): pl.pallas_call(functools.partial(multiply_body, other, parts), in_specs=[...  5.34 us
    pallas_call x2, Pallas kernels, prepare(): pl.pallas_call(functools.partial(prepare_body, stride, own_slots, chunks,...  4.37 us
    pallas_call x4, Pallas kernels, finish(): pl.pallas_call(functools.partial(finish_body, first), in_specs=[WHOLE] *...  3.61 us
  transfers between devices with their start and end apart: 20, of which 11 were waited for; matrix products, arithmetic and copies ran while one was open for 0% of the time, Pallas kernels for 27%

profile of v5, /device:TPU:0, one launch (start us, length us, event | category | flops | bytes accessed | tf_op | source)
XLA Modules:
  0.0 77.9 jit_solution(1560973812864902739)
XLA Ops:
  0.0 1.9 %prepare.3 = (bf16[160,512]{1,0:T(8,128)(2,1)S(1)}, bf16[160,512]{1,0:T(8,128)(2,1)S(1)}, bf16[160,512]{1,0:T(8,128)(2,1)S(1)}, bf16[160,512]{1,0:T(8,128)(2,1)S(1)}) custom-call(s32[16]{0:T(128)} %owner_hbm.3, f32[640]{0:T(1024)} %gauss_hbm.3, s32[160]{0:T(256)} %points_hbm.3, bf16[160,8192]{1,0:T(8,128)(2,1)} %source.3), custom_call_target="tpu_custom_call" | custom-call | flops 1 | bytes 1 | tf_op jit(solution)/shard_map/prepare/pallas_call | solution.py:141
  1.9 3.1 %collective-permute-start = (bf16[160,512]{1,0:T(8,128)(2,1)S(1)}, bf16[160,512]{1,0:T(8,128)(2,1)S(1)}, u32[]{:S(2)}, u32[]{:S(2)}) collective-permute-start(bf16[160,512]{1,0:T(8,128)(2,1)S(1)} %get-tuple-element.67), channel_id=1, source_target_pairs={{0,4},{4,0},{8,12},{12,8},{1,5},{5,1},{9,13},{13,9},{2,6},{6,2},{1... | collective-permute-start | bytes 491528 | tf_op jit(solution)/shard_map/wave_1/ppermute | solution.py:60
  5.0 2.6 %collective-permute-start.1 = (bf16[160,512]{1,0:T(8,128)(2,1)S(1)}, bf16[160,512]{1,0:T(8,128)(2,1)S(1)}, u32[]{:S(2)}, u32[]{:S(2)}) collective-permute-start(bf16[160,512]{1,0:T(8,128)(2,1)S(1)} %get-tuple-element.68), channel_id=1, source_target_pairs={{0,8},{4,12},{8,0},{12,4},{1,9},{5,13},{9,1},{13,5},{2,10},{6,14},... | collective-permute-start | bytes 491528 | tf_op jit(solution)/shard_map/wave_2/ppermute | solution.py:60
  7.6 2.4 %prepare.2 = (bf16[160,512]{1,0:T(8,128)(2,1)S(1)}, bf16[160,512]{1,0:T(8,128)(2,1)S(1)}, bf16[160,512]{1,0:T(8,128)(2,1)S(1)}, bf16[160,512]{1,0:T(8,128)(2,1)S...) custom-call(s32[16]{0:T(128)} %owner_hbm.3, ...), custom_call_target="tpu_custom_call" | custom-call | flops 1 | bytes 1 | tf_op jit(solution)/shard_map/prepare/pallas_call | solution.py:141
  11.0 3.0 %collective-permute-start.7 = (bf16[160,512]{1,0:T(8,128)(2,1)S(1)}, bf16[160,512]{1,0:T(8,128)(2,1)S(1)}, u32[]{:S(2)}, u32[]{:S(2)}) collective-permute-start(bf16[160,512]{1,0:T(8,128)(2,1)S(1)} %get-tuple-element.81), channel_id=1, source_target_pairs={{0,12},{4,8},{8,4},{12,0},{1,13},{5,9},{9,5},{13,1},{2,14},{6,10},... | collective-permute-start | bytes 491528 | tf_op jit(solution)/shard_map/wave_3/ppermute | solution.py:60
  14.0 2.7 %turn.6.refs_0_ = bf16[1280,640]{1,0:T(8,128)(2,1)S(1)} custom-call(bf16[4,640,1280]{2,1,0:T(8,128)(2,1)} %table_hbm.3), custom_call_target="tpu_custom_call" | custom-call | flops 1 | bytes 1 | tf_op jit(solution)/shard_map/turn/pallas_call | solution.py:177
  16.7 2.7 %turn.4.refs_0_ = bf16[1280,640]{1,0:T(8,128)(2,1)S(1)} custom-call(bf16[4,640,1280]{2,1,0:T(8,128)(2,1)} %table_hbm.3), custom_call_target="tpu_custom_call" | custom-call | flops 1 | bytes 1 | tf_op jit(solution)/shard_map/turn/pallas_call | solution.py:177
  21.5 5.2 %collective-permute-done.7.refs_4_ = bf16[160,512]{1,0:T(8,128)(2,1)S(1)} collective-permute-done((bf16[160,512]{1,0:T(8,128)(2,1)S(1)}, bf16[160,512]{1,0:T(8,128)(2,1)S(1)}, u32[]{:S(2)}, u32[]{:S(2)}) %collective-permute-start.7) | collective-permute-done | bytes 163872 | tf_op jit(solution)/shard_map/wave_3/ppermute | solution.py:60
  26.8 9.5 %collective-permute-done.6.refs_3_ = bf16[160,512]{1,0:T(8,128)(2,1)S(1)} collective-permute-done((bf16[160,512]{1,0:T(8,128)(2,1)S(1)}, bf16[160,512]{1,0:T(8,128)(2,1)S(1)}, u32[]{:S(2)}, u32[]{:S(2)}) %collective-permute-start.6) | collective-permute-done | bytes 163872 | tf_op jit(solution)/shard_map/wave_2/ppermute | solution.py:60
  37.1 2.5 %collective-permute-start.12 = (bf16[160,512]{1,0:T(8,128)(2,1)S(1)}, bf16[160,512]{1,0:T(8,128)(2,1)S(1)}, u32[]{:S(2)}, u32[]{:S(2)}) collective-permute-start(bf16[160,512]{1,0:T(8,128)(2,1)S(1)} %get-tuple-element.92), channel_id=1, source_target_pairs={{0,12},{4,8},{8,4},{12,0},{1,13},{5,9},{9,5},{13,1},{2,14},{6,10},... | collective-permute-start | bytes 491528 | tf_op jit(solution)/shard_map/wave_3/ppermute | solution.py:60
  39.6 1.9 %collective-permute-start.11 = (bf16[160,512]{1,0:T(8,128)(2,1)S(1)}, bf16[160,512]{1,0:T(8,128)(2,1)S(1)}, u32[]{:S(2)}, u32[]{:S(2)}) collective-permute-start(bf16[160,512]{1,0:T(8,128)(2,1)S(1)} %get-tuple-element.90), channel_id=1, source_target_pairs={{0,8},{4,12},{8,0},{12,4},{1,9},{5,13},{9,1},{13,5},{2,10},{6,14},... | collective-permute-start | bytes 491528 | tf_op jit(solution)/shard_map/wave_2/ppermute | solution.py:60
  41.5 1.5 %collective-permute-start.4 = (bf16[320,512]{1,0:T(8,128)(2,1)S(1)}, bf16[320,512]{1,0:T(8,128)(2,1)S(1)}, u32[]{:S(2)}, u32[]{:S(2)}) collective-permute-start(bf16[320,512]{1,0:T(8,128)(2,1)S(1)} %combine.4), channel_id=1, source_target_pairs={{0,2},{1,3},{2,0},{3,1},{4,6},{5,7},{6,4},{7,5},{8,10},{9,11},{10,... | collective-permute-start | bytes 983048 | tf_op jit(solution)/shard_map/lat_2/ppermute | solution.py:60
  43.7 2.7 %turn.7.refs_0_ = bf16[1280,640]{1,0:T(8,128)(2,1)S(1)} custom-call(bf16[4,640,1280]{2,1,0:T(8,128)(2,1)} %table_hbm.3), custom_call_target="tpu_custom_call" | custom-call | flops 1 | bytes 1 | tf_op jit(solution)/shard_map/turn/pallas_call | solution.py:177
  46.4 2.7 %turn.5.refs_0_ = bf16[1280,640]{1,0:T(8,128)(2,1)S(1)} custom-call(bf16[4,640,1280]{2,1,0:T(8,128)(2,1)} %table_hbm.3), custom_call_target="tpu_custom_call" | custom-call | flops 1 | bytes 1 | tf_op jit(solution)/shard_map/turn/pallas_call | solution.py:177
  50.8 1.6 %collective-permute-start.14 = (bf16[160,512]{1,0:T(8,128)(2,1)S(1)}, bf16[160,512]{1,0:T(8,128)(2,1)S(1)}, u32[]{:S(2)}, u32[]{:S(2)}) collective-permute-start(bf16[160,512]{1,0:T(8,128)(2,1)S(1)} %get-tuple-element.99), channel_id=1, source_target_pairs={{0,4},{4,0},{8,12},{12,8},{1,5},{5,1},{9,13},{13,9},{2,6},{6,2},{1... | collective-permute-start | bytes 491528 | tf_op jit(solution)/shard_map/wave_1/ppermute | solution.py:60
  53.3 1.4 %collective-permute-start.16 = (bf16[160,512]{1,0:T(8,128)(2,1)S(1)}, bf16[160,512]{1,0:T(8,128)(2,1)S(1)}, u32[]{:S(2)}, u32[]{:S(2)}) collective-permute-start(bf16[160,512]{1,0:T(8,128)(2,1)S(1)} %get-tuple-element.103), channel_id=1, source_target_pairs={{0,12},{4,8},{8,4},{12,0},{1,13},{5,9},{9,5},{13,1},{2,14},{6,10},... | collective-permute-start | bytes 491528 | tf_op jit(solution)/shard_map/wave_3/ppermute | solution.py:60
  54.7 1.3 %collective-permute-start.9 = (bf16[320,512]{1,0:T(8,128)(2,1)S(1)}, bf16[320,512]{1,0:T(8,128)(2,1)S(1)}, u32[]{:S(2)}, u32[]{:S(2)}) collective-permute-start(bf16[320,512]{1,0:T(8,128)(2,1)S(1)} %combine.5), channel_id=1, source_target_pairs={{0,2},{1,3},{2,0},{3,1},{4,6},{5,7},{6,4},{7,5},{8,10},{9,11},{10,... | collective-permute-start | bytes 983048 | tf_op jit(solution)/shard_map/lat_2/ppermute | solution.py:60
  56.0 1.3 %collective-permute-done.11.refs_3_ = bf16[160,512]{1,0:T(8,128)(2,1)S(1)} collective-permute-done((bf16[160,512]{1,0:T(8,128)(2,1)S(1)}, bf16[160,512]{1,0:T(8,128)(2,1)S(1)}, u32[]{:S(2)}, u32[]{:S(2)}) %collective-permute-start.11) | collective-permute-done | bytes 163872 | tf_op jit(solution)/shard_map/wave_2/ppermute | solution.py:60
  58.7 1.4 %collective-permute-done.13.got_ref.near_ref = bf16[2,320,512]{2,1,0:T(8,128)(2,1)S(1)} collective-permute-done((bf16[2,320,512]{2,1,0:T(8,128)(2,1)S(1)}, bf16[2,320,512]{2,1,0:T(8,128)(2,1)S(1)}, u32[]{:S(2)}, u32[]{:S(2)}) %collective-permute-start.13) | collective-permute-done | bytes 655392 | tf_op jit(solution)/shard_map/lat_1/ppermute | solution.py:60
  60.2 1.6 %collective-permute-start.19 = (bf16[320,512]{1,0:T(8,128)(2,1)S(1)}, bf16[320,512]{1,0:T(8,128)(2,1)S(1)}, u32[]{:S(2)}, u32[]{:S(2)}) collective-permute-start(bf16[320,512]{1,0:T(8,128)(2,1)S(1)} %combine.6), channel_id=1, source_target_pairs={{0,2},{1,3},{2,0},{3,1},{4,6},{5,7},{6,4},{7,5},{8,10},{9,11},{10,... | collective-permute-start | bytes 983048 | tf_op jit(solution)/shard_map/lat_2/ppermute | solution.py:60
  65.8 1.4 %collective-permute-done.17.got_ref.near_ref = bf16[2,320,512]{2,1,0:T(8,128)(2,1)S(1)} collective-permute-done((bf16[2,320,512]{2,1,0:T(8,128)(2,1)S(1)}, bf16[2,320,512]{2,1,0:T(8,128)(2,1)S(1)}, u32[]{:S(2)}, u32[]{:S(2)}) %collective-permute-start.17) | collective-permute-done | bytes 655392 | tf_op jit(solution)/shard_map/lat_1/ppermute | solution.py:60
  67.2 1.6 %collective-permute-start.18 = (bf16[320,512]{1,0:T(8,128)(2,1)S(1)}, bf16[320,512]{1,0:T(8,128)(2,1)S(1)}, u32[]{:S(2)}, u32[]{:S(2)}) collective-permute-start(bf16[320,512]{1,0:T(8,128)(2,1)S(1)} %combine.7), channel_id=1, source_target_pairs={{0,2},{1,3},{2,0},{3,1},{4,6},{5,7},{6,4},{7,5},{8,10},{9,11},{10,... | collective-permute-start | bytes 983048 | tf_op jit(solution)/shard_map/lat_2/ppermute | solution.py:60
  68.8 1.2 %collective-permute-done.19.far_ref = bf16[320,512]{1,0:T(8,128)(2,1)S(1)} collective-permute-done((bf16[320,512]{1,0:T(8,128)(2,1)S(1)}, bf16[320,512]{1,0:T(8,128)(2,1)S(1)}, u32[]{:S(2)}, u32[]{:S(2)}) %collective-permute-start.19) | collective-permute-done | bytes 327712 | tf_op jit(solution)/shard_map/lat_2/ppermute | solution.py:60
  70.9 6.1 %collective-permute-done.18.far_ref = bf16[320,512]{1,0:T(8,128)(2,1)S(1)} collective-permute-done((bf16[320,512]{1,0:T(8,128)(2,1)S(1)}, bf16[320,512]{1,0:T(8,128)(2,1)S(1)}, u32[]{:S(2)}, u32[]{:S(2)}) %collective-permute-start.18) | collective-permute-done | bytes 327712 | tf_op jit(solution)/shard_map/lat_2/ppermute | solution.py:60
  (38 shorter events, 14.3 us)
Async XLA Ops:
  1.9 17.5 %collective-permute-start = (bf16[160,512]{1,0:T(8,128)(2,1)S(1)}, bf16[160,512]{1,0:T(8,128)(2,1)S(1)}, u32[]{:S(2)}, u32[]{:S(2)}) collective-permute-start(bf16[160,512]{1,0:T(8,128)(2,1)S(1)} %get-tuple-element.67), channel_id=1, source_target_pairs={{0,4},{4,0},{8,12},{12,8},{1,5},{5,1},{9,13},{13,9},{2,6},{6,2},{1... | collective-permute-start | bytes 491528 | tf_op jit(solution)/shard_map/wave_1/ppermute | solution.py:60
  5.0 15.1 %collective-permute-start.1 = (bf16[160,512]{1,0:T(8,128)(2,1)S(1)}, bf16[160,512]{1,0:T(8,128)(2,1)S(1)}, u32[]{:S(2)}, u32[]{:S(2)}) collective-permute-start(bf16[160,512]{1,0:T(8,128)(2,1)S(1)} %get-tuple-element.68), channel_id=1, source_target_pairs={{0,8},{4,12},{8,0},{12,4},{1,9},{5,13},{9,1},{13,5},{2,10},{6,14},... | collective-permute-start | bytes 491528 | tf_op jit(solution)/shard_map/wave_2/ppermute | solution.py:60
  7.6 12.5 %collective-permute-start.2 = (bf16[160,512]{1,0:T(8,128)(2,1)S(1)}, bf16[160,512]{1,0:T(8,128)(2,1)S(1)}, u32[]{:S(2)}, u32[]{:S(2)}) collective-permute-start(bf16[160,512]{1,0:T(8,128)(2,1)S(1)} %get-tuple-element.69), channel_id=1, source_target_pairs={{0,12},{4,8},{8,4},{12,0},{1,13},{5,9},{9,5},{13,1},{2,14},{6,10},... | collective-permute-start | bytes 491528 | tf_op jit(solution)/shard_map/wave_3/ppermute | solution.py:60
  10.1 26.2 %collective-permute-start.5 = (bf16[160,512]{1,0:T(8,128)(2,1)S(1)}, bf16[160,512]{1,0:T(8,128)(2,1)S(1)}, u32[]{:S(2)}, u32[]{:S(2)}) collective-permute-start(bf16[160,512]{1,0:T(8,128)(2,1)S(1)} %get-tuple-element.79), channel_id=1, source_target_pairs={{0,4},{4,0},{8,12},{12,8},{1,5},{5,1},{9,13},{13,9},{2,6},{6,2},{1... | collective-permute-start | bytes 491528 | tf_op jit(solution)/shard_map/wave_1/ppermute | solution.py:60
  11.0 15.7 %collective-permute-start.7 = (bf16[160,512]{1,0:T(8,128)(2,1)S(1)}, bf16[160,512]{1,0:T(8,128)(2,1)S(1)}, u32[]{:S(2)}, u32[]{:S(2)}) collective-permute-start(bf16[160,512]{1,0:T(8,128)(2,1)S(1)} %get-tuple-element.81), channel_id=1, source_target_pairs={{0,12},{4,8},{8,4},{12,0},{1,13},{5,9},{9,5},{13,1},{2,14},{6,10},... | collective-permute-start | bytes 491528 | tf_op jit(solution)/shard_map/wave_3/ppermute | solution.py:60
  19.5 16.8 %collective-permute-start.6 = (bf16[160,512]{1,0:T(8,128)(2,1)S(1)}, bf16[160,512]{1,0:T(8,128)(2,1)S(1)}, u32[]{:S(2)}, u32[]{:S(2)}) collective-permute-start(bf16[160,512]{1,0:T(8,128)(2,1)S(1)} %get-tuple-element.80), channel_id=1, source_target_pairs={{0,8},{4,12},{8,0},{12,4},{1,9},{5,13},{9,1},{13,5},{2,10},{6,14},... | collective-permute-start | bytes 491528 | tf_op jit(solution)/shard_map/wave_2/ppermute | solution.py:60
  20.8 15.5 %collective-permute-start.3 = (bf16[2,320,512]{2,1,0:T(8,128)(2,1)S(1)}, bf16[2,320,512]{2,1,0:T(8,128)(2,1)S(1)}, u32[]{:S(2)}, u32[]{:S(2)}) collective-permute-start(bf16[2,320,512]{2,1,0:T(8,128)(2,1)S(1)} %multiply_other.4), channel_id=1, source_target_pairs={{0,1},{1,0},{2,3},{3,2},{4,5},{5,4},{6,7},{7,6},{8,9},{9,8},{10,11... | collective-permute-start | bytes 1966088 | tf_op jit(solution)/shard_map/lat_1/ppermute | solution.py:60
  36.9 12.2 %collective-permute-start.8 = (bf16[2,320,512]{2,1,0:T(8,128)(2,1)S(1)}, bf16[2,320,512]{2,1,0:T(8,128)(2,1)S(1)}, u32[]{:S(2)}, u32[]{:S(2)}) collective-permute-start(bf16[2,320,512]{2,1,0:T(8,128)(2,1)S(1)} %multiply_other.5), channel_id=1, source_target_pairs={{0,1},{1,0},{2,3},{3,2},{4,5},{5,4},{6,7},{7,6},{8,9},{9,8},{10,11... | collective-permute-start | bytes 1966088 | tf_op jit(solution)/shard_map/lat_1/ppermute | solution.py:60
  37.1 16.2 %collective-permute-start.12 = (bf16[160,512]{1,0:T(8,128)(2,1)S(1)}, bf16[160,512]{1,0:T(8,128)(2,1)S(1)}, u32[]{:S(2)}, u32[]{:S(2)}) collective-permute-start(bf16[160,512]{1,0:T(8,128)(2,1)S(1)} %get-tuple-element.92), channel_id=1, source_target_pairs={{0,12},{4,8},{8,4},{12,0},{1,13},{5,9},{9,5},{13,1},{2,14},{6,10},... | collective-permute-start | bytes 491528 | tf_op jit(solution)/shard_map/wave_3/ppermute | solution.py:60
  39.6 15.1 %collective-permute-start.10 = (bf16[160,512]{1,0:T(8,128)(2,1)S(1)}, bf16[160,512]{1,0:T(8,128)(2,1)S(1)}, u32[]{:S(2)}, u32[]{:S(2)}) collective-permute-start(bf16[160,512]{1,0:T(8,128)(2,1)S(1)} %get-tuple-element.89), channel_id=1, source_target_pairs={{0,4},{4,0},{8,12},{12,8},{1,5},{5,1},{9,13},{13,9},{2,6},{6,2},{1... | collective-permute-start | bytes 491528 | tf_op jit(solution)/shard_map/wave_1/ppermute | solution.py:60
  39.6 17.7 %collective-permute-start.11 = (bf16[160,512]{1,0:T(8,128)(2,1)S(1)}, bf16[160,512]{1,0:T(8,128)(2,1)S(1)}, u32[]{:S(2)}, u32[]{:S(2)}) collective-permute-start(bf16[160,512]{1,0:T(8,128)(2,1)S(1)} %get-tuple-element.90), channel_id=1, source_target_pairs={{0,8},{4,12},{8,0},{12,4},{1,9},{5,13},{9,1},{13,5},{2,10},{6,14},... | collective-permute-start | bytes 491528 | tf_op jit(solution)/shard_map/wave_2/ppermute | solution.py:60
  41.5 9.3 %collective-permute-start.4 = (bf16[320,512]{1,0:T(8,128)(2,1)S(1)}, bf16[320,512]{1,0:T(8,128)(2,1)S(1)}, u32[]{:S(2)}, u32[]{:S(2)}) collective-permute-start(bf16[320,512]{1,0:T(8,128)(2,1)S(1)} %combine.4), channel_id=1, source_target_pairs={{0,2},{1,3},{2,0},{3,1},{4,6},{5,7},{6,4},{7,5},{8,10},{9,11},{10,... | collective-permute-start | bytes 983048 | tf_op jit(solution)/shard_map/lat_2/ppermute | solution.py:60
  49.1 15.2 %collective-permute-start.15 = (bf16[160,512]{1,0:T(8,128)(2,1)S(1)}, bf16[160,512]{1,0:T(8,128)(2,1)S(1)}, u32[]{:S(2)}, u32[]{:S(2)}) collective-permute-start(bf16[160,512]{1,0:T(8,128)(2,1)S(1)} %get-tuple-element.101), channel_id=1, source_target_pairs={{0,8},{4,12},{8,0},{12,4},{1,9},{5,13},{9,1},{13,5},{2,10},{6,14},... | collective-permute-start | bytes 491528 | tf_op jit(solution)/shard_map/wave_2/ppermute | solution.py:60
  50.8 13.5 %collective-permute-start.14 = (bf16[160,512]{1,0:T(8,128)(2,1)S(1)}, bf16[160,512]{1,0:T(8,128)(2,1)S(1)}, u32[]{:S(2)}, u32[]{:S(2)}) collective-permute-start(bf16[160,512]{1,0:T(8,128)(2,1)S(1)} %get-tuple-element.99), channel_id=1, source_target_pairs={{0,4},{4,0},{8,12},{12,8},{1,5},{5,1},{9,13},{13,9},{2,6},{6,2},{1... | collective-permute-start | bytes 491528 | tf_op jit(solution)/shard_map/wave_1/ppermute | solution.py:60
  53.3 11.0 %collective-permute-start.16 = (bf16[160,512]{1,0:T(8,128)(2,1)S(1)}, bf16[160,512]{1,0:T(8,128)(2,1)S(1)}, u32[]{:S(2)}, u32[]{:S(2)}) collective-permute-start(bf16[160,512]{1,0:T(8,128)(2,1)S(1)} %get-tuple-element.103), channel_id=1, source_target_pairs={{0,12},{4,8},{8,4},{12,0},{1,13},{5,9},{9,5},{13,1},{2,14},{6,10},... | collective-permute-start | bytes 491528 | tf_op jit(solution)/shard_map/wave_3/ppermute | solution.py:60
  54.7 8.1 %collective-permute-start.9 = (bf16[320,512]{1,0:T(8,128)(2,1)S(1)}, bf16[320,512]{1,0:T(8,128)(2,1)S(1)}, u32[]{:S(2)}, u32[]{:S(2)}) collective-permute-start(bf16[320,512]{1,0:T(8,128)(2,1)S(1)} %combine.5), channel_id=1, source_target_pairs={{0,2},{1,3},{2,0},{3,1},{4,6},{5,7},{6,4},{7,5},{8,10},{9,11},{10,... | collective-permute-start | bytes 983048 | tf_op jit(solution)/shard_map/lat_2/ppermute | solution.py:60
  58.0 2.2 %collective-permute-start.13 = (bf16[2,320,512]{2,1,0:T(8,128)(2,1)S(1)}, bf16[2,320,512]{2,1,0:T(8,128)(2,1)S(1)}, u32[]{:S(2)}, u32[]{:S(2)}) collective-permute-start(bf16[2,320,512]{2,1,0:T(8,128)(2,1)S(1)} %multiply_other.6), channel_id=1, source_target_pairs={{0,1},{1,0},{2,3},{3,2},{4,5},{5,4},{6,7},{7,6},{8,9},{9,8},{10,11... | collective-permute-start | bytes 1966088 | tf_op jit(solution)/shard_map/lat_1/ppermute | solution.py:60
  60.2 9.8 %collective-permute-start.19 = (bf16[320,512]{1,0:T(8,128)(2,1)S(1)}, bf16[320,512]{1,0:T(8,128)(2,1)S(1)}, u32[]{:S(2)}, u32[]{:S(2)}) collective-permute-start(bf16[320,512]{1,0:T(8,128)(2,1)S(1)} %combine.6), channel_id=1, source_target_pairs={{0,2},{1,3},{2,0},{3,1},{4,6},{5,7},{6,4},{7,5},{8,10},{9,11},{10,... | collective-permute-start | bytes 983048 | tf_op jit(solution)/shard_map/lat_2/ppermute | solution.py:60
  65.0 2.2 %collective-permute-start.17 = (bf16[2,320,512]{2,1,0:T(8,128)(2,1)S(1)}, bf16[2,320,512]{2,1,0:T(8,128)(2,1)S(1)}, u32[]{:S(2)}, u32[]{:S(2)}) collective-permute-start(bf16[2,320,512]{2,1,0:T(8,128)(2,1)S(1)} %multiply_other.7), channel_id=1, source_target_pairs={{0,1},{1,0},{2,3},{3,2},{4,5},{5,4},{6,7},{7,6},{8,9},{9,8},{10,11... | collective-permute-start | bytes 1966088 | tf_op jit(solution)/shard_map/lat_1/ppermute | solution.py:60
  67.2 9.8 %collective-permute-start.18 = (bf16[320,512]{1,0:T(8,128)(2,1)S(1)}, bf16[320,512]{1,0:T(8,128)(2,1)S(1)}, u32[]{:S(2)}, u32[]{:S(2)}) collective-permute-start(bf16[320,512]{1,0:T(8,128)(2,1)S(1)} %combine.7), channel_id=1, source_target_pairs={{0,2},{1,3},{2,0},{3,1},{4,6},{5,7},{6,4},{7,5},{8,10},{9,11},{10,... | collective-permute-start | bytes 983048 | tf_op jit(solution)/shard_map/lat_2/ppermute | solution.py:60
